TPU v7x, 32 devices: a whole 2x2x4 slice. The times are simulated.
32 devices in a mesh: shot: 4 (over x, core), slab: 8 (over z, y).
Axes of the slice: x: 2, y: 2, z: 4, core: 2. Of those that a mesh axis runs over, the one named last changes fastest.
Arguments:
- lame_lambda: float32 [16, 32, 128], P('slab'), may hold values from 0.5 to 1.5
- lame_mu: float32 [16, 32, 128], P('slab'), may hold values from 0.3 to 0.8
- buoyancy: float32 [16, 32, 128], P('slab'), may hold values from 0.5 to 1
- forward_state: float32 [4, 9, 16, 32, 128], P('shot', None, 'slab'), may hold values from -6 to 6
- adjoint_state: float32 [4, 9, 16, 32, 128], P('shot', None, 'slab'), may hold values from -6 to 6
- source_wavelet: float32 [4, 8], P('shot'), may hold values from -20 to 20
- source_cell: int32 [4], P('shot'), may hold values from 0 to 65535
- residual_traces: float32 [4, 8, 1024], P('shot', None, 'slab'), may hold values from -12 to 12
- receiver_slab: int32 [1024, 1], P('slab'), may hold values from 0 to 7; in each aligned block of 128 rows (0 to 127, 128 to 255, ...) at most 32 rows name the same one
- receiver_cell: int32 [1024], P('slab'), may hold values from 0 to 8191
Outputs:
- adjoint_start: float32 [4, 9, 16, 32, 128], P('shot', None, 'slab')
- lambda_gradient: float32 [16, 32, 128], P('slab', 'shot')
- mu_gradient: float32 [16, 32, 128], P('slab', 'shot')
Inputs may be any that keep to these rules, and one draw needn't show every extreme that they name: `receiver_slab`: among the 128 receivers held by one index of slab, at most 32 lie in any one slab.
All inputs are finite; a program needn't handle non-finite values.
Results may differ from a plain program's by a relative error of at most 0.000067.
Values sent between devices are 32-bit elements; how exact they have to be, the bound alone decides.
A program may use at most 64 MiB of HBM per device.

v0:
```python
import jax
import jax.numpy as jnp
from jax import lax
from jax.sharding import PartitionSpec as P

TIME_STEP = 0.3


def from_behind(value, axis, steps):
    count = lax.axis_size(axis)
    initial, last = (max(0, -steps), min(count, count - steps))
    return lax.ppermute(value, axis, [(source, source + steps) for source in range(initial, last)])


def next_cell(values, along):
    extent = values.shape[along]
    remainder = lax.slice_in_dim(values, 1, extent, axis=along)
    border = jnp.zeros_like(lax.slice_in_dim(values, 0, 1, axis=along))
    return jnp.concatenate([remainder, border], axis=along)


def prev_cell(values, along):
    extent = values.shape[along]
    remainder = lax.slice_in_dim(values, 0, extent - 1, axis=along)
    border = jnp.zeros_like(lax.slice_in_dim(values, 0, 1, axis=along))
    return jnp.concatenate([border, remainder], axis=along)


def velocity_update(velocity, stress, buoyancy, normal_after, shear_before):
    sigma_xx = stress[:, 0]
    sigma_yy = stress[:, 1]
    sigma_zz = stress[:, 2]
    sigma_xy = stress[:, 3]
    sigma_xz = stress[:, 4]
    sigma_yz = stress[:, 5]
    accel_x = (
        normal_after
        - sigma_xx
        + (sigma_xy - prev_cell(sigma_xy, 2))
        + (sigma_xz - prev_cell(sigma_xz, 3))
    )
    accel_y = (
        sigma_xy
        - shear_before[:, 0]
        + (next_cell(sigma_yy, 2) - sigma_yy)
        + (sigma_yz - prev_cell(sigma_yz, 3))
    )
    accel_z = (
        sigma_xz
        - shear_before[:, 1]
        + (sigma_yz - prev_cell(sigma_yz, 2))
        + (next_cell(sigma_zz, 3) - sigma_zz)
    )
    factor = TIME_STEP * buoyancy
    return jnp.stack(
        [
            velocity[:, 0] - factor * accel_x,
            velocity[:, 1] - factor * accel_y,
            velocity[:, 2] - factor * accel_z,
        ],
        axis=1,
    )


def stress_update(velocity, stress, lame_lambda, lame_mu, speed_before, speeds_after):
    speed_x = velocity[:, 0]
    speed_y = velocity[:, 1]
    speed_z = velocity[:, 2]
    strain_xx = speed_x - speed_before[:, 0]
    strain_yy = speed_y - prev_cell(speed_y, 2)
    strain_zz = speed_z - prev_cell(speed_z, 3)
    strain_xy = next_cell(speed_x, 2) - speed_x + (speeds_after[:, 0] - speed_y)
    strain_xz = next_cell(speed_x, 3) - speed_x + (speeds_after[:, 1] - speed_z)
    strain_yz = next_cell(speed_y, 3) - speed_y + (next_cell(speed_z, 2) - speed_z)
    dilation = strain_xx + strain_yy + strain_zz
    volume_term = lame_lambda * dilation
    twice_mu = 2.0 * lame_mu
    updated = jnp.stack(
        [
            stress[:, 0] - TIME_STEP * (volume_term + twice_mu * strain_xx),
            stress[:, 1] - TIME_STEP * (volume_term + twice_mu * strain_yy),
            stress[:, 2] - TIME_STEP * (volume_term + twice_mu * strain_zz),
            stress[:, 3] - TIME_STEP * (lame_mu * strain_xy),
            stress[:, 4] - TIME_STEP * (lame_mu * strain_xz),
            stress[:, 5] - TIME_STEP * (lame_mu * strain_yz),
        ],
        axis=1,
    )
    return (updated, (strain_xx, strain_yy, strain_zz, strain_xy, strain_xz, strain_yz))


def imaging(strains):
    strain_xx, strain_yy, strain_zz, strain_xy, strain_xz, strain_yz = strains
    dilation = strain_xx + strain_yy + strain_zz
    lambda_term = TIME_STEP * (dilation[0] * dilation[1])
    shear_term = 2.0 * (
        strain_xx[0] * strain_xx[1] + strain_yy[0] * strain_yy[1] + strain_zz[0] * strain_zz[1]
    )
    shear_term = (
        shear_term
        + strain_xy[0] * strain_xy[1]
        + strain_xz[0] * strain_xz[1]
        + strain_yz[0] * strain_yz[1]
    )
    return (lambda_term, TIME_STEP * shear_term)


def shards(
    lame_lambda,
    lame_mu,
    buoyancy,
    forward_state,
    adjoint_state,
    source_wavelet,
    source_cell,
    residual_traces,
    receiver_slab,
    receiver_cell,
):
    planes, rows_y, depth = lame_lambda.shape
    cell_count = planes * rows_y * depth
    steps_total = source_wavelet.shape[1]
    my_slab = lax.axis_index("slab")
    traces = residual_traces[0]
    target_slab = receiver_slab[:, 0]
    targets = (target_slab * cell_count + receiver_cell).astype(jnp.float32)[None, :]
    arrived, landing = (
        lax.all_gather(traces, "slab", axis=1, tiled=True),
        lax.all_gather(targets, "slab", axis=1, tiled=True),
    )
    local_cell = landing[0].astype(jnp.int32) - my_slab * cell_count
    usable = (local_cell >= 0) & (local_cell < cell_count)
    cell_index = jnp.where(usable, local_cell, 0)
    amounts = jnp.where(usable[None, :], arrived, 0.0)
    receiver_push = jnp.zeros((steps_total, cell_count), jnp.float32).at[:, cell_index].add(amounts)
    receiver_push = receiver_push.reshape(steps_total, planes, rows_y, depth)
    source_local = source_cell[0] - my_slab * cell_count
    source_spot = (
        (jnp.arange(cell_count, dtype=jnp.int32) == source_local)
        .astype(jnp.float32)
        .reshape(planes, rows_y, depth)
    )
    wavefields = jnp.concatenate([forward_state, adjoint_state], axis=0)
    grad_lambda = jnp.zeros((planes, rows_y, depth), jnp.float32)
    grad_shear = jnp.zeros((planes, rows_y, depth), jnp.float32)
    for step_index in range(steps_total):
        stress_now = wavefields[:, 3:9]
        normal_next = from_behind(stress_now[:, 0, 0:1], "slab", -1)
        shear_prev = from_behind(stress_now[:, 3:5, planes - 1 : planes], "slab", 1)
        normal_after = jnp.concatenate([stress_now[:, 0, 1:], normal_next], axis=1)
        shear_before = jnp.concatenate([shear_prev, stress_now[:, 3:5, : planes - 1]], axis=2)
        velocity = velocity_update(
            wavefields[:, 0:3], stress_now, buoyancy, normal_after, shear_before
        )
        speed_prev = from_behind(velocity[:, 0:1, planes - 1 : planes], "slab", 1)
        speed_next = from_behind(velocity[:, 1:3, 0:1], "slab", -1)
        speed_before = jnp.concatenate([speed_prev, velocity[:, 0:1, : planes - 1]], axis=2)
        speeds_after = jnp.concatenate([velocity[:, 1:3, 1:], speed_next], axis=2)
        stress, strains = stress_update(
            velocity, stress_now, lame_lambda, lame_mu, speed_before, speeds_after
        )
        lambda_term, shear_term = imaging(strains)
        grad_lambda = grad_lambda + lambda_term
        grad_shear = grad_shear + shear_term
        pushes = jnp.stack([source_spot * source_wavelet[0, step_index], receiver_push[step_index]])
        stress = stress.at[:, 0:3].add(-TIME_STEP * pushes[:, None])
        wavefields = jnp.concatenate([velocity, stress], axis=1)
    lambda_part, shear_part = (
        lax.psum_scatter(grad_lambda, "shot", scatter_dimension=1, tiled=True),
        lax.psum_scatter(grad_shear, "shot", scatter_dimension=1, tiled=True),
    )
    return (wavefields[1:2], lambda_part, shear_part)


def solution(mesh):
    in_specs = (
        P("slab", None, None),
        P("slab", None, None),
        P("slab", None, None),
        P("shot", None, "slab", None, None),
        P("shot", None, "slab", None, None),
        P("shot", None),
        P("shot"),
        P("shot", None, "slab"),
        P("slab", None),
        P("slab"),
    )
    out_specs = (
        P("shot", None, "slab", None, None),
        P("slab", "shot", None),
        P("slab", "shot", None),
    )
    return jax.shard_map(shards, mesh=mesh, in_specs=in_specs, out_specs=out_specs, check_vma=False)
```

profile of v0, /device:TPU:11, one launch (start us, length us, event | category | flops | bytes accessed | tf_op | source)
XLA Modules:
  0.0 297.1 jit_solution(13675962574684482571)
XLA Ops:
  8.0 3.1 %collective-permute-start.2 = (f32[2,2,1,32,128]{4,3,0,2,1:T(8,128)S(1)}, f32[2,2,1,32,128]{4,3,0,2,1:T(8,128)S(1)}, u32[]{:S(2)}, u32[]{:S(2)}) collective-permute-start(f32[2,2,1,32,128]{4,3,0,2,1:T(8,128)S(1)} %get-tuple-element.218), channel_id=1, source_target_pairs={{0,1},{1,2},{2,3},{3,4},{4,5},{5,6},{6,7},{8,9},{9,10},{10,11},{11... | collective-permute-start | bytes 196616 | tf_op jit(solution)/shard_map/ppermute | solution.py:12
  12.0 3.0 %collective-permute-start = (f32[2,1,32,128]{3,2,0,1:T(8,128)S(1)}, f32[2,1,32,128]{3,2,0,1:T(8,128)S(1)}, u32[]{:S(2)}, u32[]{:S(2)}) collective-permute-start(f32[2,1,32,128]{3,2,0,1:T(8,128)S(1)} %get-tuple-element.213), channel_id=1, source_target_pairs={{1,0},{2,1},{3,2},{4,3},{5,4},{6,5},{7,6},{9,8},{10,9},{11,10},{12... | collective-permute-start | bytes 98312 | tf_op jit(solution)/shard_map/ppermute | solution.py:12
  20.4 13.2 %all-gather.2 = f32[8,1,128]{2,1,0:T(1,128)S(1)} all-gather(f32[1,1,128]{2,1,0:T(1,128)S(1)} %fusion.300), channel_id=2, replica_groups=mesh['shot'=4,'slab'=8] {'slab'}, dimensions={0}, use_global_device_ids=true | all-gather | bytes 4608 | tf_op jit(solution)/shard_map/all_gather | solution.py:129
  33.7 24.2 %all-gather.1 = f32[1,8,1024]{2,1,0:T(8,128)S(1)} all-gather(f32[1,8,128]{2,1,0:T(8,128)} %param.33), channel_id=3, replica_groups=mesh['shot'=4,'slab'=8] {'slab'}, dimensions={2}, use_global_device_ids=true | all-gather | bytes 36864 | tf_op jit(solution)/shard_map/all_gather | solution.py:128
  58.1 9.4 %scatter_custom_fusion = f32[8,8192]{0,1:T(8,128)} fusion(s32[1024]{0:T(1024)S(1)} %bitcast.957, f32[1024,8]{1,0:T(8,128)S(1)} %copy.267, f32[]{:T(128)} %constant.207.clone.1), kind=kCustom, calls=%fused_computation.9 | custom fusion | flops 8192 | bytes 262148 | tf_op jit(solution)/shard_map/scatter-add | solution.py:135
  67.5 28.9 %slice_reduce_fusion = (f32[8192]{0:T(1024)}, f32[8192]{0:T(1024)S(1)}, f32[8192]{0:T(1024)S(1)}, f32[8192]{0:T(1024)S(1)}, f32[8192]{0:T(1024)S(1)}, /*index=5*...) fusion(f32[8,8192]{0,1:T(8,128)} %scatter_custom_fusion), kind=kLoop, calls=%fused_computation.1 | loop fusion | bytes 524288 | tf_op jit(solution)/shard_map/slice | solution.py:165
  103.3 4.3 %collective-permute-start.4 = (f32[2,2,1,32,128]{4,3,0,2,1:T(8,128)S(1)}, f32[2,2,1,32,128]{4,3,0,2,1:T(8,128)S(1)}, u32[]{:S(2)}, u32[]{:S(2)}) collective-permute-start(f32[2,2,1,32,128]{4,3,0,2,1:T(8,128)S(1)} %get-tuple-element.332), channel_id=1, source_target_pairs={{1,0},{2,1},{3,2},{4,3},{5,4},{6,5},{7,6},{9,8},{10,9},{11,10},{12... | collective-permute-start | bytes 196616 | tf_op jit(solution)/shard_map/ppermute | solution.py:12
  108.4 3.3 %collective-permute-start.3 = (f32[2,1,32,128]{3,2,0,1:T(8,128)S(1)}, f32[2,1,32,128]{3,2,0,1:T(8,128)S(1)}, u32[]{:S(2)}, u32[]{:S(2)}) collective-permute-start(f32[2,1,32,128]{3,2,0,1:T(8,128)S(1)} %get-tuple-element.311), channel_id=1, source_target_pairs={{1,0},{2,1},{3,2},{4,3},{5,4},{6,5},{7,6},{9,8},{10,9},{11,10},{12... | collective-permute-start | bytes 98312 | tf_op jit(solution)/shard_map/ppermute | solution.py:12
  118.0 2.7 collective-permute-start.8
  123.2 3.4 %collective-permute-start.7 = (f32[2,1,32,128]{3,2,0,1:T(8,128)S(1)}, f32[2,1,32,128]{3,2,0,1:T(8,128)S(1)}, u32[]{:S(2)}, u32[]{:S(2)}) collective-permute-start(f32[2,1,32,128]{3,2,0,1:T(8,128)S(1)} %get-tuple-element.307), channel_id=1, source_target_pairs={{1,0},{2,1},{3,2},{4,3},{5,4},{6,5},{7,6},{9,8},{10,9},{11,10},{12... | collective-permute-start | bytes 98312 | tf_op jit(solution)/shard_map/ppermute | solution.py:12
  128.9 3.6 %collective-permute-start.9 = (f32[2,1,1,32,128]{4,3,0,2,1:T(8,128)S(1)}, f32[2,1,1,32,128]{4,3,0,2,1:T(8,128)S(1)}, u32[]{:S(2)}, u32[]{:S(2)}) collective-permute-start(f32[2,1,1,32,128]{4,3,0,2,1:T(8,128)S(1)} %get-tuple-element.353), channel_id=1, source_target_pairs={{0,1},{1,2},{2,3},{3,4},{4,5},{5,6},{6,7},{8,9},{9,10},{10,11},{11... | collective-permute-start | bytes 98312 | tf_op jit(solution)/shard_map/ppermute | solution.py:12
  135.5 3.0 %collective-permute-done.12 = f32[2,2,1,32,128]{4,3,0,2,1:T(8,128)S(1)} collective-permute-done((f32[2,2,1,32,128]{4,3,0,2,1:T(8,128)S(1)}, f32[2,2,1,32,128]{4,3,0,2,1:T(8,128)S(1)}, u32[]{:S(2)}, u32[]{:S(2)}) %collective-permute-start.12) | collective-permute-done | bytes 65568 | tf_op jit(solution)/shard_map/ppermute | solution.py:12
  138.7 2.8 collective-permute-start.11
  141.6 2.5 collective-permute-start.14
  144.3 3.3 %collective-permute-start.13 = (f32[2,1,1,32,128]{4,3,0,2,1:T(8,128)S(1)}, f32[2,1,1,32,128]{4,3,0,2,1:T(8,128)S(1)}, u32[]{:S(2)}, u32[]{:S(2)}) collective-permute-start(f32[2,1,1,32,128]{4,3,0,2,1:T(8,128)S(1)} %get-tuple-element.351), channel_id=1, source_target_pairs={{0,1},{1,2},{2,3},{3,4},{4,5},{5,6},{6,7},{8,9},{9,10},{10,11},{11... | collective-permute-start | bytes 98312 | tf_op jit(solution)/shard_map/ppermute | solution.py:12
  148.3 2.4 collective-permute-start.16
  150.8 2.5 collective-permute-done.16
  153.6 4.2 %collective-permute-start.15 = (f32[2,1,32,128]{3,2,0,1:T(8,128)S(1)}, f32[2,1,32,128]{3,2,0,1:T(8,128)S(1)}, u32[]{:S(2)}, u32[]{:S(2)}) collective-permute-start(f32[2,1,32,128]{3,2,0,1:T(8,128)S(1)} %get-tuple-element.299), channel_id=1, source_target_pairs={{1,0},{2,1},{3,2},{4,3},{5,4},{6,5},{7,6},{9,8},{10,9},{11,10},{12... | collective-permute-start | bytes 98312 | tf_op jit(solution)/shard_map/ppermute | solution.py:12
  159.9 3.5 %collective-permute-start.17 = (f32[2,1,1,32,128]{4,3,0,2,1:T(8,128)S(1)}, f32[2,1,1,32,128]{4,3,0,2,1:T(8,128)S(1)}, u32[]{:S(2)}, u32[]{:S(2)}) collective-permute-start(f32[2,1,1,32,128]{4,3,0,2,1:T(8,128)S(1)} %get-tuple-element.349), channel_id=1, source_target_pairs={{0,1},{1,2},{2,3},{3,4},{4,5},{5,6},{6,7},{8,9},{9,10},{10,11},{11... | collective-permute-start | bytes 98312 | tf_op jit(solution)/shard_map/ppermute | solution.py:12
  164.0 2.3 collective-permute-start.20
  169.8 2.8 collective-permute-start.22
  173.4 3.3 %collective-permute-start.19 = (f32[2,1,32,128]{3,2,1,0:T(8,128)S(1)}, f32[2,1,32,128]{3,2,1,0:T(8,128)S(1)}, u32[]{:S(2)}, u32[]{:S(2)}) collective-permute-start(f32[2,1,32,128]{3,2,1,0:T(8,128)S(1)} %get-tuple-element.295), channel_id=1, source_target_pairs={{1,0},{2,1},{3,2},{4,3},{5,4},{6,5},{7,6},{9,8},{10,9},{11,10},{12... | collective-permute-start | bytes 98312 | tf_op jit(solution)/shard_map/ppermute | solution.py:12
  178.3 4.2 %collective-permute-start.24 = (f32[2,2,1,32,128]{4,3,2,0,1:T(8,128)S(1)}, f32[2,2,1,32,128]{4,3,2,0,1:T(8,128)S(1)}, u32[]{:S(2)}, u32[]{:S(2)}) collective-permute-start(f32[2,2,1,32,128]{4,3,2,0,1:T(8,128)S(1)} %get-tuple-element.322), channel_id=1, source_target_pairs={{1,0},{2,1},{3,2},{4,3},{5,4},{6,5},{7,6},{9,8},{10,9},{11,10},{12... | collective-permute-start | bytes 196616 | tf_op jit(solution)/shard_map/ppermute | solution.py:12
  185.3 2.9 collective-permute-done.21
  191.2 4.3 %collective-permute-start.23 = (f32[2,1,32,128]{3,2,0,1:T(8,128)S(1)}, f32[2,1,32,128]{3,2,0,1:T(8,128)S(1)}, u32[]{:S(2)}, u32[]{:S(2)}) collective-permute-start(f32[2,1,32,128]{3,2,0,1:T(8,128)S(1)} %get-tuple-element.290), channel_id=1, source_target_pairs={{1,0},{2,1},{3,2},{4,3},{5,4},{6,5},{7,6},{9,8},{10,9},{11,10},{12... | collective-permute-start | bytes 98312 | tf_op jit(solution)/shard_map/ppermute | solution.py:12
  197.3 4.0 %collective-permute-start.28 = (f32[2,2,1,32,128]{4,3,2,0,1:T(8,128)S(1)}, f32[2,2,1,32,128]{4,3,2,0,1:T(8,128)S(1)}, u32[]{:S(2)}, u32[]{:S(2)}) collective-permute-start(f32[2,2,1,32,128]{4,3,2,0,1:T(8,128)S(1)} %get-tuple-element.320), channel_id=1, source_target_pairs={{1,0},{2,1},{3,2},{4,3},{5,4},{6,5},{7,6},{9,8},{10,9},{11,10},{12... | collective-permute-start | bytes 196616 | tf_op jit(solution)/shard_map/ppermute | solution.py:12
  204.0 2.9 collective-permute-done.25
  209.6 3.4 %collective-permute-start.29 = (f32[2,2,1,32,128]{4,3,2,0,1:T(8,128)S(1)}, f32[2,2,1,32,128]{4,3,2,0,1:T(8,128)S(1)}, u32[]{:S(2)}, u32[]{:S(2)}) collective-permute-start(f32[2,2,1,32,128]{4,3,2,0,1:T(8,128)S(1)} %fusion.16), channel_id=1, source_target_pairs={{0,1},{1,2},{2,3},{3,4},{4,5},{5,6},{6,7},{8,9},{9,10},{10,11},{11... | collective-permute-start | bytes 196616 | tf_op jit(solution)/shard_map/ppermute | solution.py:12
  214.5 2.8 collective-permute-start.30
  219.5 3.3 %collective-permute-start.31 = (f32[2,2,1,32,128]{4,3,2,0,1:T(8,128)}, f32[2,2,1,32,128]{4,3,2,0,1:T(8,128)}, u32[]{:S(2)}, u32[]{:S(2)}) collective-permute-start(f32[2,2,1,32,128]{4,3,2,0,1:T(8,128)} %get-tuple-element.318), channel_id=1, source_target_pairs={{1,0},{2,1},{3,2},{4,3},{5,4},{6,5},{7,6},{9,8},{10,9},{11,10},{12... | collective-permute-start | bytes 196616 | tf_op jit(solution)/shard_map/ppermute | solution.py:12
  230.7 37.1 %reduce-scatter.3.cloned.1.call-done = f32[2,8,128]{2,1,0:T(8,128)} async-done(((f32[2,32,128]{2,1,0:T(8,128)}), f32[2,8,128]{2,1,0:T(8,128)}) %reduce-scatter.3.cloned.1.call-update) | async-done | bytes 8208 | tf_op jit(solution)/shard_map/reduce_scatter | solution.py:169
  267.8 22.5 %reduce-scatter.5.cloned.1.call-done = f32[2,8,128]{2,1,0:T(8,128)} async-done(((f32[2,32,128]{2,1,0:T(8,128)}), f32[2,8,128]{2,1,0:T(8,128)}) %reduce-scatter.5.cloned.1.call-update) | async-done | bytes 8208 | tf_op jit(solution)/shard_map/reduce_scatter | solution.py:170
  (225 shorter events, 61.9 us)
Async XLA Ops:
  7.2 260.6 %reduce-scatter.3.cloned.1.call-start = ((), (), s32[]{:S(2)}) async-start(), calls=%async_computation.2 | async-start | bytes 40960 | tf_op jit(solution)/shard_map/reduce_scatter | solution.py:169
  8.0 92.8 %collective-permute-start.2 = (f32[2,2,1,32,128]{4,3,0,2,1:T(8,128)S(1)}, f32[2,2,1,32,128]{4,3,0,2,1:T(8,128)S(1)}, u32[]{:S(2)}, u32[]{:S(2)}) collective-permute-start(f32[2,2,1,32,128]{4,3,0,2,1:T(8,128)S(1)} %get-tuple-element.218), channel_id=1, source_target_pairs={{0,1},{1,2},{2,3},{3,4},{4,5},{5,6},{6,7},{8,9},{9,10},{10,11},{11... | collective-permute-start | bytes 196616 | tf_op jit(solution)/shard_map/ppermute | solution.py:12
  12.0 89.1 %collective-permute-start = (f32[2,1,32,128]{3,2,0,1:T(8,128)S(1)}, f32[2,1,32,128]{3,2,0,1:T(8,128)S(1)}, u32[]{:S(2)}, u32[]{:S(2)}) collective-permute-start(f32[2,1,32,128]{3,2,0,1:T(8,128)S(1)} %get-tuple-element.213), channel_id=1, source_target_pairs={{1,0},{2,1},{3,2},{4,3},{5,4},{6,5},{7,6},{9,8},{10,9},{11,10},{12... | collective-permute-start | bytes 98312 | tf_op jit(solution)/shard_map/ppermute | solution.py:12
  101.2 6.4 %collective-permute-start.1 = (f32[2,1,1,32,128]{4,3,0,2,1:T(8,128)S(1)}, f32[2,1,1,32,128]{4,3,0,2,1:T(8,128)S(1)}, u32[]{:S(2)}, u32[]{:S(2)}) collective-permute-start(f32[2,1,1,32,128]{4,3,0,2,1:T(8,128)S(1)} %get-tuple-element.357), channel_id=1, source_target_pairs={{0,1},{1,2},{2,3},{3,4},{4,5},{5,6},{6,7},{8,9},{9,10},{10,11},{11... | collective-permute-start | bytes 98312 | tf_op jit(solution)/shard_map/ppermute | solution.py:12
  103.3 8.4 %collective-permute-start.4 = (f32[2,2,1,32,128]{4,3,0,2,1:T(8,128)S(1)}, f32[2,2,1,32,128]{4,3,0,2,1:T(8,128)S(1)}, u32[]{:S(2)}, u32[]{:S(2)}) collective-permute-start(f32[2,2,1,32,128]{4,3,0,2,1:T(8,128)S(1)} %get-tuple-element.332), channel_id=1, source_target_pairs={{1,0},{2,1},{3,2},{4,3},{5,4},{6,5},{7,6},{9,8},{10,9},{11,10},{12... | collective-permute-start | bytes 196616 | tf_op jit(solution)/shard_map/ppermute | solution.py:12
  108.4 5.5 %collective-permute-start.3 = (f32[2,1,32,128]{3,2,0,1:T(8,128)S(1)}, f32[2,1,32,128]{3,2,0,1:T(8,128)S(1)}, u32[]{:S(2)}, u32[]{:S(2)}) collective-permute-start(f32[2,1,32,128]{3,2,0,1:T(8,128)S(1)} %get-tuple-element.311), channel_id=1, source_target_pairs={{1,0},{2,1},{3,2},{4,3},{5,4},{6,5},{7,6},{9,8},{10,9},{11,10},{12... | collective-permute-start | bytes 98312 | tf_op jit(solution)/shard_map/ppermute | solution.py:12
  111.9 5.9 %collective-permute-start.6 = (f32[2,2,1,32,128]{4,3,0,2,1:T(8,128)S(1)}, f32[2,2,1,32,128]{4,3,0,2,1:T(8,128)S(1)}, u32[]{:S(2)}, u32[]{:S(2)}) collective-permute-start(f32[2,2,1,32,128]{4,3,0,2,1:T(8,128)S(1)} %fusion.52), channel_id=1, source_target_pairs={{0,1},{1,2},{2,3},{3,4},{4,5},{5,6},{6,7},{8,9},{9,10},{10,11},{11... | collective-permute-start | bytes 196616 | tf_op jit(solution)/shard_map/ppermute | solution.py:12
  114.1 6.7 %collective-permute-start.5 = (f32[2,1,1,32,128]{4,3,0,2,1:T(8,128)S(1)}, f32[2,1,1,32,128]{4,3,0,2,1:T(8,128)S(1)}, u32[]{:S(2)}, u32[]{:S(2)}) collective-permute-start(f32[2,1,1,32,128]{4,3,0,2,1:T(8,128)S(1)} %get-tuple-element.355), channel_id=1, source_target_pairs={{0,1},{1,2},{2,3},{3,4},{4,5},{5,6},{6,7},{8,9},{9,10},{10,11},{11... | collective-permute-start | bytes 98312 | tf_op jit(solution)/shard_map/ppermute | solution.py:12
  118.0 5.0 %collective-permute-start.8 = (f32[2,2,1,32,128]{4,3,0,2,1:T(8,128)S(1)}, f32[2,2,1,32,128]{4,3,0,2,1:T(8,128)S(1)}, u32[]{:S(2)}, u32[]{:S(2)}) collective-permute-start(f32[2,2,1,32,128]{4,3,0,2,1:T(8,128)S(1)} %get-tuple-element.330), channel_id=1, source_target_pairs={{1,0},{2,1},{3,2},{4,3},{5,4},{6,5},{7,6},{9,8},{10,9},{11,10},{12... | collective-permute-start | bytes 196616 | tf_op jit(solution)/shard_map/ppermute | solution.py:12
  123.2 5.5 %collective-permute-start.7 = (f32[2,1,32,128]{3,2,0,1:T(8,128)S(1)}, f32[2,1,32,128]{3,2,0,1:T(8,128)S(1)}, u32[]{:S(2)}, u32[]{:S(2)}) collective-permute-start(f32[2,1,32,128]{3,2,0,1:T(8,128)S(1)} %get-tuple-element.307), channel_id=1, source_target_pairs={{1,0},{2,1},{3,2},{4,3},{5,4},{6,5},{7,6},{9,8},{10,9},{11,10},{12... | collective-permute-start | bytes 98312 | tf_op jit(solution)/shard_map/ppermute | solution.py:12
  126.8 6.5 %collective-permute-start.10 = (f32[2,2,1,32,128]{4,3,0,2,1:T(8,128)S(1)}, f32[2,2,1,32,128]{4,3,0,2,1:T(8,128)S(1)}, u32[]{:S(2)}, u32[]{:S(2)}) collective-permute-start(f32[2,2,1,32,128]{4,3,0,2,1:T(8,128)S(1)} %fusion.46), channel_id=1, source_target_pairs={{0,1},{1,2},{2,3},{3,4},{4,5},{5,6},{6,7},{8,9},{9,10},{10,11},{11... | collective-permute-start | bytes 196616 | tf_op jit(solution)/shard_map/ppermute | solution.py:12
  128.9 6.5 %collective-permute-start.9 = (f32[2,1,1,32,128]{4,3,0,2,1:T(8,128)S(1)}, f32[2,1,1,32,128]{4,3,0,2,1:T(8,128)S(1)}, u32[]{:S(2)}, u32[]{:S(2)}) collective-permute-start(f32[2,1,1,32,128]{4,3,0,2,1:T(8,128)S(1)} %get-tuple-element.353), channel_id=1, source_target_pairs={{0,1},{1,2},{2,3},{3,4},{4,5},{5,6},{6,7},{8,9},{9,10},{10,11},{11... | collective-permute-start | bytes 98312 | tf_op jit(solution)/shard_map/ppermute | solution.py:12
  133.5 5.0 %collective-permute-start.12 = (f32[2,2,1,32,128]{4,3,0,2,1:T(8,128)S(1)}, f32[2,2,1,32,128]{4,3,0,2,1:T(8,128)S(1)}, u32[]{:S(2)}, u32[]{:S(2)}) collective-permute-start(f32[2,2,1,32,128]{4,3,0,2,1:T(8,128)S(1)} %get-tuple-element.328), channel_id=1, source_target_pairs={{1,0},{2,1},{3,2},{4,3},{5,4},{6,5},{7,6},{9,8},{10,9},{11,10},{12... | collective-permute-start | bytes 196616 | tf_op jit(solution)/shard_map/ppermute | solution.py:12
  138.7 5.4 %collective-permute-start.11 = (f32[2,1,32,128]{3,2,0,1:T(8,128)S(1)}, f32[2,1,32,128]{3,2,0,1:T(8,128)S(1)}, u32[]{:S(2)}, u32[]{:S(2)}) collective-permute-start(f32[2,1,32,128]{3,2,0,1:T(8,128)S(1)} %get-tuple-element.303), channel_id=1, source_target_pairs={{1,0},{2,1},{3,2},{4,3},{5,4},{6,5},{7,6},{9,8},{10,9},{11,10},{12... | collective-permute-start | bytes 98312 | tf_op jit(solution)/shard_map/ppermute | solution.py:12
  141.6 6.5 %collective-permute-start.14 = (f32[2,2,1,32,128]{4,3,0,2,1:T(8,128)S(1)}, f32[2,2,1,32,128]{4,3,0,2,1:T(8,128)S(1)}, u32[]{:S(2)}, u32[]{:S(2)}) collective-permute-start(f32[2,2,1,32,128]{4,3,0,2,1:T(8,128)S(1)} %fusion.40), channel_id=1, source_target_pairs={{0,1},{1,2},{2,3},{3,4},{4,5},{5,6},{6,7},{8,9},{9,10},{10,11},{11... | collective-permute-start | bytes 196616 | tf_op jit(solution)/shard_map/ppermute | solution.py:12
  144.3 6.5 %collective-permute-start.13 = (f32[2,1,1,32,128]{4,3,0,2,1:T(8,128)S(1)}, f32[2,1,1,32,128]{4,3,0,2,1:T(8,128)S(1)}, u32[]{:S(2)}, u32[]{:S(2)}) collective-permute-start(f32[2,1,1,32,128]{4,3,0,2,1:T(8,128)S(1)} %get-tuple-element.351), channel_id=1, source_target_pairs={{0,1},{1,2},{2,3},{3,4},{4,5},{5,6},{6,7},{8,9},{9,10},{10,11},{11... | collective-permute-start | bytes 98312 | tf_op jit(solution)/shard_map/ppermute | solution.py:12
  148.3 5.0 %collective-permute-start.16 = (f32[2,2,1,32,128]{4,3,0,2,1:T(8,128)S(1)}, f32[2,2,1,32,128]{4,3,0,2,1:T(8,128)S(1)}, u32[]{:S(2)}, u32[]{:S(2)}) collective-permute-start(f32[2,2,1,32,128]{4,3,0,2,1:T(8,128)S(1)} %get-tuple-element.326), channel_id=1, source_target_pairs={{1,0},{2,1},{3,2},{4,3},{5,4},{6,5},{7,6},{9,8},{10,9},{11,10},{12... | collective-permute-start | bytes 196616 | tf_op jit(solution)/shard_map/ppermute | solution.py:12
  153.6 6.3 %collective-permute-start.15 = (f32[2,1,32,128]{3,2,0,1:T(8,128)S(1)}, f32[2,1,32,128]{3,2,0,1:T(8,128)S(1)}, u32[]{:S(2)}, u32[]{:S(2)}) collective-permute-start(f32[2,1,32,128]{3,2,0,1:T(8,128)S(1)} %get-tuple-element.299), channel_id=1, source_target_pairs={{1,0},{2,1},{3,2},{4,3},{5,4},{6,5},{7,6},{9,8},{10,9},{11,10},{12... | collective-permute-start | bytes 98312 | tf_op jit(solution)/shard_map/ppermute | solution.py:12
  157.9 5.9 %collective-permute-start.18 = (f32[2,2,1,32,128]{4,3,0,2,1:T(8,128)S(1)}, f32[2,2,1,32,128]{4,3,0,2,1:T(8,128)S(1)}, u32[]{:S(2)}, u32[]{:S(2)}) collective-permute-start(f32[2,2,1,32,128]{4,3,0,2,1:T(8,128)S(1)} %fusion.34), channel_id=1, source_target_pairs={{0,1},{1,2},{2,3},{3,4},{4,5},{5,6},{6,7},{8,9},{9,10},{10,11},{11... | collective-permute-start | bytes 196616 | tf_op jit(solution)/shard_map/ppermute | solution.py:12
  159.9 7.2 %collective-permute-start.17 = (f32[2,1,1,32,128]{4,3,0,2,1:T(8,128)S(1)}, f32[2,1,1,32,128]{4,3,0,2,1:T(8,128)S(1)}, u32[]{:S(2)}, u32[]{:S(2)}) collective-permute-start(f32[2,1,1,32,128]{4,3,0,2,1:T(8,128)S(1)} %get-tuple-element.349), channel_id=1, source_target_pairs={{0,1},{1,2},{2,3},{3,4},{4,5},{5,6},{6,7},{8,9},{9,10},{10,11},{11... | collective-permute-start | bytes 98312 | tf_op jit(solution)/shard_map/ppermute | solution.py:12
  169.8 6.9 %collective-permute-start.22 = (f32[2,2,1,32,128]{4,3,2,0,1:T(8,128)S(1)}, f32[2,2,1,32,128]{4,3,2,0,1:T(8,128)S(1)}, u32[]{:S(2)}, u32[]{:S(2)}) collective-permute-start(f32[2,2,1,32,128]{4,3,2,0,1:T(8,128)S(1)} %fusion.28), channel_id=1, source_target_pairs={{0,1},{1,2},{2,3},{3,4},{4,5},{5,6},{6,7},{8,9},{9,10},{10,11},{11... | collective-permute-start | bytes 196616 | tf_op jit(solution)/shard_map/ppermute | solution.py:12
  178.3 9.9 %collective-permute-start.24 = (f32[2,2,1,32,128]{4,3,2,0,1:T(8,128)S(1)}, f32[2,2,1,32,128]{4,3,2,0,1:T(8,128)S(1)}, u32[]{:S(2)}, u32[]{:S(2)}) collective-permute-start(f32[2,2,1,32,128]{4,3,2,0,1:T(8,128)S(1)} %get-tuple-element.322), channel_id=1, source_target_pairs={{1,0},{2,1},{3,2},{4,3},{5,4},{6,5},{7,6},{9,8},{10,9},{11,10},{12... | collective-permute-start | bytes 196616 | tf_op jit(solution)/shard_map/ppermute | solution.py:12
  182.5 5.7 %collective-permute-start.21 = (f32[2,1,1,32,128]{4,3,2,0,1:T(8,128)S(1)}, f32[2,1,1,32,128]{4,3,2,0,1:T(8,128)S(1)}, u32[]{:S(2)}, u32[]{:S(2)}) collective-permute-start(f32[2,1,1,32,128]{4,3,2,0,1:T(8,128)S(1)} %get-tuple-element.346), channel_id=1, source_target_pairs={{0,1},{1,2},{2,3},{3,4},{4,5},{5,6},{6,7},{8,9},{9,10},{10,11},{11... | collective-permute-start | bytes 98312 | tf_op jit(solution)/shard_map/ppermute | solution.py:12
  189.1 6.3 %collective-permute-start.26 = (f32[2,2,1,32,128]{4,3,2,0,1:T(8,128)S(1)}, f32[2,2,1,32,128]{4,3,2,0,1:T(8,128)S(1)}, u32[]{:S(2)}, u32[]{:S(2)}) collective-permute-start(f32[2,2,1,32,128]{4,3,2,0,1:T(8,128)S(1)} %fusion.22), channel_id=1, source_target_pairs={{0,1},{1,2},{2,3},{3,4},{4,5},{5,6},{6,7},{8,9},{9,10},{10,11},{11... | collective-permute-start | bytes 196616 | tf_op jit(solution)/shard_map/ppermute | solution.py:12
  191.2 5.8 %collective-permute-start.23 = (f32[2,1,32,128]{3,2,0,1:T(8,128)S(1)}, f32[2,1,32,128]{3,2,0,1:T(8,128)S(1)}, u32[]{:S(2)}, u32[]{:S(2)}) collective-permute-start(f32[2,1,32,128]{3,2,0,1:T(8,128)S(1)} %get-tuple-element.290), channel_id=1, source_target_pairs={{1,0},{2,1},{3,2},{4,3},{5,4},{6,5},{7,6},{9,8},{10,9},{11,10},{12... | collective-permute-start | bytes 98312 | tf_op jit(solution)/shard_map/ppermute | solution.py:12
  197.3 9.6 %collective-permute-start.28 = (f32[2,2,1,32,128]{4,3,2,0,1:T(8,128)S(1)}, f32[2,2,1,32,128]{4,3,2,0,1:T(8,128)S(1)}, u32[]{:S(2)}, u32[]{:S(2)}) collective-permute-start(f32[2,2,1,32,128]{4,3,2,0,1:T(8,128)S(1)} %get-tuple-element.320), channel_id=1, source_target_pairs={{1,0},{2,1},{3,2},{4,3},{5,4},{6,5},{7,6},{9,8},{10,9},{11,10},{12... | collective-permute-start | bytes 196616 | tf_op jit(solution)/shard_map/ppermute | solution.py:12
  201.3 5.6 %collective-permute-start.25 = (f32[2,1,1,32,128]{4,3,2,0,1:T(8,128)S(1)}, f32[2,1,1,32,128]{4,3,2,0,1:T(8,128)S(1)}, u32[]{:S(2)}, u32[]{:S(2)}) collective-permute-start(f32[2,1,1,32,128]{4,3,2,0,1:T(8,128)S(1)} %get-tuple-element.342), channel_id=1, source_target_pairs={{0,1},{1,2},{2,3},{3,4},{4,5},{5,6},{6,7},{8,9},{9,10},{10,11},{11... | collective-permute-start | bytes 98312 | tf_op jit(solution)/shard_map/ppermute | solution.py:12
  207.7 5.4 %collective-permute-start.27 = (f32[2,1,32,128]{3,2,1,0:T(8,128)S(1)}, f32[2,1,32,128]{3,2,1,0:T(8,128)S(1)}, u32[]{:S(2)}, u32[]{:S(2)}) collective-permute-start(f32[2,1,32,128]{3,2,1,0:T(8,128)S(1)} %get-tuple-element.284), channel_id=1, source_target_pairs={{1,0},{2,1},{3,2},{4,3},{5,4},{6,5},{7,6},{9,8},{10,9},{11,10},{12... | collective-permute-start | bytes 98312 | tf_op jit(solution)/shard_map/ppermute | solution.py:12
  209.6 7.8 %collective-permute-start.29 = (f32[2,2,1,32,128]{4,3,2,0,1:T(8,128)S(1)}, f32[2,2,1,32,128]{4,3,2,0,1:T(8,128)S(1)}, u32[]{:S(2)}, u32[]{:S(2)}) collective-permute-start(f32[2,2,1,32,128]{4,3,2,0,1:T(8,128)S(1)} %fusion.16), channel_id=1, source_target_pairs={{0,1},{1,2},{2,3},{3,4},{4,5},{5,6},{6,7},{8,9},{9,10},{10,11},{11... | collective-permute-start | bytes 196616 | tf_op jit(solution)/shard_map/ppermute | solution.py:12
  214.5 8.3 %collective-permute-start.30 = (f32[2,1,1,32,128]{4,3,2,0,1:T(8,128)S(1)}, f32[2,1,1,32,128]{4,3,2,0,1:T(8,128)S(1)}, u32[]{:S(2)}, u32[]{:S(2)}) collective-permute-start(f32[2,1,1,32,128]{4,3,2,0,1:T(8,128)S(1)} %get-tuple-element.340), channel_id=1, source_target_pairs={{0,1},{1,2},{2,3},{3,4},{4,5},{5,6},{6,7},{8,9},{9,10},{10,11},{11... | collective-permute-start | bytes 98312 | tf_op jit(solution)/shard_map/ppermute | solution.py:12
  219.5 5.5 %collective-permute-start.31 = (f32[2,2,1,32,128]{4,3,2,0,1:T(8,128)}, f32[2,2,1,32,128]{4,3,2,0,1:T(8,128)}, u32[]{:S(2)}, u32[]{:S(2)}) collective-permute-start(f32[2,2,1,32,128]{4,3,2,0,1:T(8,128)} %get-tuple-element.318), channel_id=1, source_target_pairs={{1,0},{2,1},{3,2},{4,3},{5,4},{6,5},{7,6},{9,8},{10,9},{11,10},{12... | collective-permute-start | bytes 196616 | tf_op jit(solution)/shard_map/ppermute | solution.py:12
  223.6 66.6 %reduce-scatter.5.cloned.1.call-start = ((), (), s32[]{:S(2)}) async-start(), calls=%async_computation.3 | async-start | bytes 40960 | tf_op jit(solution)/shard_map/reduce_scatter | solution.py:170
  (10 other events, 138.5 us)
Sparse Core Ops, SparseCore 0:
  223.7 43.9 reduce-scatter.2
  270.9 19.3 reduce-scatter.4
where the time goes:
time: 302 us; the launch traced here: 297 us
  starting transfers between devices  92 us (30%)
  waiting for transfers between devices  81.2 us (27%)
  blocking collectives  37.4 us (12%)
  local copies, waits for them, and re-layouts  35.6 us (12%)
  other arithmetic  35 us (12%)
  between operations  16 us (5%)
    ppermute x32, starting transfers between devices, from_behind(): lax.ppermute(value, axis, [(source, source + steps) for source in range(i...  91.9 us
    reduce_scatter x1, waiting for transfers between devices, shards(): lax.psum_scatter(grad_lambda, 'shot', scatter_dimension=1, tiled=True)  37.1 us
    slice x1, local copies, waits for them, and re-layouts, shards(): receiver_push[step_index]  28.9 us
    all_gather x1, blocking collectives, shards(): lax.all_gather(traces, 'slab', axis=1, tiled=True)  24.2 us
    reduce_scatter x1, waiting for transfers between devices, shards(): lax.psum_scatter(grad_shear, 'shot', scatter_dimension=1, tiled=True)  22.5 us
    ppermute x32, waiting for transfers between devices, from_behind(): lax.ppermute(value, axis, [(source, source + steps) for source in range(i...  21.6 us
    all_gather x1, blocking collectives, shards(): lax.all_gather(targets, 'slab', axis=1, tiled=True)  13.2 us
    scatter-add x1, other arithmetic, shards(): jnp.zeros((steps_total, cell_count), jnp.float32).at[:, cell_index]  9.37 us
  transfers between devices with their start and end apart: 34, of which 14 were waited for; matrix products, arithmetic and copies ran while one was open for 22% of the time, Pallas kernels for 0%

commit v1 on v0

v1 whole, which is shorter than its diff:
```python
import functools
import jax
import jax.numpy as jnp
from jax import lax
from jax.experimental import pallas as pl
from jax.experimental.pallas import tpu as pltpu
from jax.sharding import PartitionSpec as P

DT = 0.3
MESH = pl.DeviceIdType.MESH
MSG = 16


def at_virtual(shot, slab):
    core, half = lax.rem(shot, 2), lax.rem(slab, 2)
    return (shot - core + half, slab - half + core)


def kernel(
    n_shot,
    n_slab,
    steps,
    lam_hbm,
    mu_hbm,
    buo_hbm,
    fwd_hbm,
    adj_hbm,
    wavelet_ref,
    source_ref,
    traces_ref,
    rslab_ref,
    rcell_ref,
    adj_out,
    lam_out,
    mu_out,
    st,
    par,
    edge,
    edge_par,
    rx_s,
    rx_v,
    tx_s,
    tx_v,
    msg,
    rx_msg,
    push,
    spot,
    amp,
    grad,
    rx_grad,
    in_send,
    in_recv,
    edge_send,
    edge_recv,
    s_send,
    s_recv,
    v_send,
    v_recv,
    msg_send,
    msg_recv,
    grad_send,
    grad_recv,
    out_send,
    out_recv,
):
    ny, nz = st.shape[3], st.shape[4]
    cells = 2 * ny * nz
    rows = 2 * ny
    shot, slab = lax.axis_index("shot"), lax.axis_index("slab")
    my_shot, my_slab = at_virtual(shot, slab)
    stays = lax.rem(shot, 2) == lax.rem(slab, 2)
    moves = jnp.logical_not(stays)
    partner = (my_shot, my_slab)
    prev_dev = at_virtual(my_shot, jnp.maximum(my_slab - 1, 0))
    next_dev = at_virtual(my_shot, jnp.minimum(my_slab + 1, n_slab - 1))
    has_prev, has_next = my_slab > 0, my_slab < n_slab - 1

    def remote(src, dst, ssem, rsem, dev):
        return pltpu.make_async_remote_copy(
            src_ref=src, dst_ref=dst, send_sem=ssem, recv_sem=rsem, device_id=dev, device_id_type=MESH
        )

    msg[...] = jnp.zeros_like(msg)
    msg[0:steps] = traces_ref[0]
    msg[steps : steps + 1] = rslab_ref[...].astype(jnp.float32)
    msg[steps + 1 : steps + 2] = rcell_ref[...].astype(jnp.float32)
    msg[steps + 2 : steps + 3, 0:steps] = wavelet_ref[...]
    msg[steps + 3 : steps + 4] = jnp.broadcast_to(source_ref[...].astype(jnp.float32), (1, 128))

    def msg_copy(t):
        return remote(msg, rx_msg.at[slab], msg_send.at[t], msg_recv.at[slab], at_virtual(shot, t))

    def msg_local():
        return pltpu.make_async_copy(msg, rx_msg.at[slab], msg_recv.at[slab])

    def is_self(t):
        return jnp.logical_and(stays, t == slab)

    def send_msg(t, carry):
        pl.when(jnp.logical_not(is_self(t)))(lambda: msg_copy(t).start())
        return carry

    lax.fori_loop(0, n_slab, send_msg, 0)
    pl.when(stays)(lambda: msg_local().start())

    orig_prev = at_virtual(shot, jnp.maximum(slab - 1, 0))
    orig_next = at_virtual(shot, jnp.minimum(slab + 1, n_slab - 1))
    to_next, to_prev = [], []
    for w, field in enumerate((fwd_hbm, adj_hbm)):
        to_next += [
            (field.at[0, 0, 1], edge.at[w, 0]),
            (field.at[0, 6:8, 1], edge.at[w, 1:3]),
            (field.at[0, 3, 1], rx_s.at[0, 0, w]),
        ]
        to_prev += [(field.at[0, 3, 0], rx_s.at[0, 1, w])]
    to_next += [(mu_hbm.at[1], edge_par.at[0]), (buo_hbm.at[1], edge_par.at[1])]
    next_copies = [
        remote(a, b, edge_send.at[i], edge_recv.at[i], orig_next) for i, (a, b) in enumerate(to_next)
    ]
    prev_copies = [
        remote(a, b, edge_send.at[8 + i], edge_recv.at[8 + i], orig_prev)
        for i, (a, b) in enumerate(to_prev)
    ]
    sends_next, sends_prev = slab < n_slab - 1, slab > 0

    @pl.when(sends_next)
    def _():
        for copy in next_copies:
            copy.start()

    @pl.when(sends_prev)
    def _():
        for copy in prev_copies:
            copy.start()

    pairs = [
        (fwd_hbm.at[0], st.at[0]),
        (adj_hbm.at[0], st.at[1]),
        (lam_hbm, par.at[0]),
        (mu_hbm, par.at[1]),
        (buo_hbm, par.at[2]),
    ]
    local_in = [pltpu.make_async_copy(a, b, in_recv.at[i]) for i, (a, b) in enumerate(pairs)]
    swap_in = [remote(a, b, in_send.at[i], in_recv.at[i], partner) for i, (a, b) in enumerate(pairs)]

    @pl.when(stays)
    def _():
        for copy in local_in:
            copy.start()

    @pl.when(moves)
    def _():
        for copy in swap_in:
            copy.start()

    @pl.when(jnp.logical_not(has_prev))
    def _():
        edge[...] = jnp.zeros_like(edge)
        edge_par[...] = jnp.zeros_like(edge_par)
        rx_s[:, 0] = jnp.zeros((steps, 2, ny, nz), jnp.float32)
        rx_v[:, 0] = jnp.zeros((steps, 2, 2, ny, nz), jnp.float32)

    @pl.when(jnp.logical_not(has_next))
    def _():
        rx_s[:, 1] = jnp.zeros((steps, 2, ny, nz), jnp.float32)
        rx_v[:, 1] = jnp.zeros((steps, 2, 2, ny, nz), jnp.float32)

    grad[...] = jnp.zeros_like(grad)
    push[...] = jnp.zeros_like(push)

    row_of = lax.broadcasted_iota(jnp.int32, (rows, 128), 0)
    col_of = lax.broadcasted_iota(jnp.int32, (nz, 128), 0)

    def scatter(q, carry):
        from_dev = at_virtual(my_shot, q)
        pltpu.make_async_copy(msg, rx_msg.at[q], msg_recv.at[q]).wait()
        block = rx_msg[q]
        named = block[steps : steps + 1].astype(jnp.int32)
        cell = block[steps + 1 : steps + 2].astype(jnp.int32)
        row = jnp.where(named == my_slab, cell // nz, -1)
        hit = row_of == row
        column = (col_of == lax.rem(cell, nz)).astype(jnp.float32).astype(jnp.bfloat16)
        trace = block[0:steps]
        high = trace.astype(jnp.bfloat16).astype(jnp.float32)
        middle = (trace - high).astype(jnp.bfloat16).astype(jnp.float32)
        low = trace - high - middle
        for k in range(steps):
            left = jnp.concatenate(
                [jnp.where(hit, part[k : k + 1], 0.0) for part in (high, middle, low)], axis=0
            ).astype(jnp.bfloat16)
            out = lax.dot_general(
                left, column, (((1,), (1,)), ((), ())), preferred_element_type=jnp.float32
            )
            push[k] += out[0:rows] + out[rows : 2 * rows] + out[2 * rows :]
        return carry

    lax.fori_loop(0, n_slab, scatter, 0)

    head = rx_msg[my_slab]
    source = head[steps + 3 : steps + 4].astype(jnp.int32) - my_slab * cells
    flat = row_of * nz + lax.broadcasted_iota(jnp.int32, (rows, nz), 1)
    spot[...] = (flat == source).astype(jnp.float32)
    for k in range(steps):
        amp[k] = jnp.broadcast_to(DT * head[steps + 2 : steps + 3, k : k + 1], (8, nz))

    @pl.when(stays)
    def _():
        for copy in local_in:
            copy.wait()

    @pl.when(moves)
    def _():
        for copy in swap_in:
            copy.wait_recv()

    @pl.when(has_prev)
    def _():
        for copy in next_copies:
            copy.wait_recv()

    @pl.when(has_next)
    def _():
        for copy in prev_copies:
            copy.wait_recv()

    y_at = lax.broadcasted_iota(jnp.int32, (ny, nz), 0)
    z_at = lax.broadcasted_iota(jnp.int32, (ny, nz), 1)

    def yn(a):
        return jnp.where(y_at < ny - 1, pltpu.roll(a, ny - 1, 0), 0.0)

    def yp(a):
        return jnp.where(y_at > 0, pltpu.roll(a, 1, 0), 0.0)

    def zn(a):
        return jnp.where(z_at < nz - 1, pltpu.roll(a, nz - 1, 1), 0.0)

    def zp(a):
        return jnp.where(z_at > 0, pltpu.roll(a, 1, 1), 0.0)

    par[0] = DT * par[0]
    par[1] = DT * par[1]
    par[2] = DT * par[2]
    edge_par[...] = DT * edge_par[...]

    def v_copies(k):
        return (
            remote(tx_v.at[k, 0], rx_v.at[k, 1], v_send.at[k, 0], v_recv.at[k, 1], prev_dev),
            remote(tx_v.at[k, 1], rx_v.at[k, 0], v_send.at[k, 1], v_recv.at[k, 0], next_dev),
        )

    def s_copies(k):
        return (
            remote(tx_s.at[k, 0], rx_s.at[k, 1], s_send.at[k, 0], s_recv.at[k, 1], prev_dev),
            remote(tx_s.at[k, 1], rx_s.at[k, 0], s_send.at[k, 1], s_recv.at[k, 0], next_dev),
        )

    def step(k, carry):
        for w in range(2):
            for i in range(2):
                sxy0 = edge[w, 1] if i == 0 else st[w, 6, 0]
                sxz0 = edge[w, 2] if i == 0 else st[w, 7, 0]
                syy, szz, syz = st[w, 4, i], st[w, 5, i], st[w, 8, i]
                vy = st[w, 1, i] - par[2, i] * (
                    (st[w, 6, i] - sxy0) + (yn(syy) - syy) + (syz - zp(syz))
                )
                vz = st[w, 2, i] - par[2, i] * (
                    (st[w, 7, i] - sxz0) + (syz - yp(syz)) + (zn(szz) - szz)
                )
                st[w, 1, i] = vy
                st[w, 2, i] = vz
                tx_v[k, i, w, 0] = vy
                tx_v[k, i, w, 1] = vz
        back, ahead = v_copies(k)
        pl.when(has_prev)(lambda: back.start())
        pl.when(has_next)(lambda: ahead.start())

        @pl.when(k > 0)
        def _():
            s_back, s_ahead = s_copies(k)
            pl.when(has_prev)(lambda: s_ahead.wait_recv())
            pl.when(has_next)(lambda: s_back.wait_recv())

        for w in range(2):
            sxx = [rx_s[k, 0, w], st[w, 3, 0], st[w, 3, 1], rx_s[k, 1, w]]
            for i in range(3):
                sxy = edge[w, 1] if i == 0 else st[w, 6, i - 1]
                sxz = edge[w, 2] if i == 0 else st[w, 7, i - 1]
                factor = edge_par[1] if i == 0 else par[2, i - 1]
                change = factor * ((sxx[i + 1] - sxx[i]) + (sxy - yp(sxy)) + (sxz - zp(sxz)))
                if i == 0:
                    edge[w, 0] = edge[w, 0] - change
                else:
                    st[w, 0, i - 1] = st[w, 0, i - 1] - change

        for i in range(2):
            terms = []
            at = pl.ds(i * ny, ny)
            gains = (amp[k, 0:1] * spot[at], DT * push[k, at])
            for w in range(2):
                vx0 = edge[w, 0] if i == 0 else st[w, 0, 0]
                vy, vz = st[w, 1, i], st[w, 2, i]
                exx = st[w, 0, i] - vx0
                eyy = vy - yp(vy)
                ezz = vz - zp(vz)
                tr = exx + eyy + ezz
                common = par[0, i] * tr + gains[w]
                twice = 2.0 * par[1, i]
                sxx = st[w, 3, i] - (common + twice * exx)
                st[w, 3, i] = sxx
                tx_s[k, i, w] = sxx
                st[w, 4, i] = st[w, 4, i] - (common + twice * eyy)
                st[w, 5, i] = st[w, 5, i] - (common + twice * ezz)
                terms.append((exx, eyy, ezz, tr))
            f, a = terms
            grad[0, i] += f[3] * a[3]
            grad[1, i] += 2.0 * (f[0] * a[0] + f[1] * a[1] + f[2] * a[2])

        @pl.when(k < steps - 1)
        def _():
            s_back = remote(
                tx_s.at[k, 0], rx_s.at[k + 1, 1], s_send.at[k, 0], s_recv.at[k + 1, 1], prev_dev
            )
            s_ahead = remote(
                tx_s.at[k, 1], rx_s.at[k + 1, 0], s_send.at[k, 1], s_recv.at[k + 1, 0], next_dev
            )
            pl.when(has_prev)(lambda: s_back.start())
            pl.when(has_next)(lambda: s_ahead.start())

        for i in range(2):
            eyz = []
            for w in range(2):
                vy, vz = st[w, 1, i], st[w, 2, i]
                strain = (zn(vy) - vy) + (yn(vz) - vz)
                st[w, 8, i] = st[w, 8, i] - par[1, i] * strain
                eyz.append(strain)
            grad[1, i] += eyz[0] * eyz[1]

        pl.when(has_prev)(lambda: ahead.wait_recv())
        pl.when(has_next)(lambda: back.wait_recv())
        for i in range(3):
            pair = []
            for w in range(2):
                vx = edge[w, 0] if i == 0 else st[w, 0, i - 1]
                vy0 = rx_v[k, 0, w, 0] if i == 0 else st[w, 1, i - 1]
                vz0 = rx_v[k, 0, w, 1] if i == 0 else st[w, 2, i - 1]
                vy1 = rx_v[k, 1, w, 0] if i == 2 else st[w, 1, i]
                vz1 = rx_v[k, 1, w, 1] if i == 2 else st[w, 2, i]
                exy = (yn(vx) - vx) + (vy1 - vy0)
                exz = (zn(vx) - vx) + (vz1 - vz0)
                if i == 0:
                    edge[w, 1] = edge[w, 1] - edge_par[0] * exy
                    edge[w, 2] = edge[w, 2] - edge_par[0] * exz
                else:
                    st[w, 6, i - 1] = st[w, 6, i - 1] - par[1, i - 1] * exy
                    st[w, 7, i - 1] = st[w, 7, i - 1] - par[1, i - 1] * exz
                pair.append((exy, exz))
            if i > 0:
                grad[1, i - 1] += pair[0][0] * pair[1][0] + pair[0][1] * pair[1][1]
        return carry

    lax.fori_loop(0, steps, step, 0)

    out_local = pltpu.make_async_copy(st.at[1], adj_out.at[0], out_recv)
    out_remote = remote(st.at[1], adj_out.at[0], out_send, out_recv, partner)

    grad[...] = DT * grad[...]
    part = ny // n_shot

    def grad_remote(t):
        return remote(
            grad.at[:, :, pl.ds(t * part, part)],
            rx_grad.at[my_shot],
            grad_send.at[t],
            grad_recv.at[my_shot],
            (jnp.int32(t), my_slab),
        )

    for t in range(n_shot):
        own = jnp.logical_and(stays, t == shot)

        @pl.when(jnp.logical_not(own))
        def _(t=t):
            grad_remote(t).start()

        @pl.when(own)
        def _(t=t):
            rx_grad[t] = grad[:, :, t * part : (t + 1) * part]

    pl.when(stays)(lambda: out_local.start())
    pl.when(moves)(lambda: out_remote.start())

    for t in range(n_shot):
        own = jnp.logical_and(stays, t == shot)

        @pl.when(jnp.logical_not(own))
        def _(t=t):
            remote(
                grad.at[:, :, pl.ds(t * part, part)],
                rx_grad.at[t],
                grad_send.at[t],
                grad_recv.at[t],
                (jnp.int32(t), my_slab),
            ).wait_recv()

    total = rx_grad[0]
    for t in range(1, n_shot):
        total = total + rx_grad[t]
    lam_out[...] = total[0]
    mu_out[...] = total[1]

    for t in range(n_shot):
        own = jnp.logical_and(stays, t == shot)
        pl.when(jnp.logical_not(own))(lambda t=t: grad_remote(t).wait_send())

    def drain(k, carry):
        back, ahead = v_copies(k)
        pl.when(has_prev)(lambda: back.wait_send())
        pl.when(has_next)(lambda: ahead.wait_send())

        @pl.when(k < steps - 1)
        def _():
            s_back, s_ahead = s_copies(k)
            pl.when(has_prev)(lambda: s_back.wait_send())
            pl.when(has_next)(lambda: s_ahead.wait_send())

        return carry

    lax.fori_loop(0, steps, drain, 0)

    def drain_msg(t, carry):
        pl.when(jnp.logical_not(is_self(t)))(lambda: msg_copy(t).wait_send())
        return carry

    lax.fori_loop(0, n_slab, drain_msg, 0)

    @pl.when(sends_next)
    def _():
        for copy in next_copies:
            copy.wait_send()

    @pl.when(sends_prev)
    def _():
        for copy in prev_copies:
            copy.wait_send()

    pl.when(stays)(lambda: out_local.wait())

    @pl.when(moves)
    def _():
        for copy in swap_in:
            copy.wait_send()
        out_remote.wait()


def shards(n_shot, n_slab, lam, mu, buo, fwd, adj, wavelet, source, traces, rslab, rcell):
    planes, ny, nz = lam.shape
    steps = wavelet.shape[1]
    nrec = traces.shape[2]
    f32 = jnp.float32
    vmem = pl.BlockSpec(memory_space=pltpu.VMEM)
    hbm = pl.BlockSpec(memory_space=pl.ANY)
    dma = pltpu.SemaphoreType.DMA
    part = ny // n_shot
    return pl.pallas_call(
        functools.partial(kernel, n_shot, n_slab, steps),
        out_shape=(
            jax.ShapeDtypeStruct((1, 9, planes, ny, nz), f32),
            jax.ShapeDtypeStruct((planes, part, nz), f32),
            jax.ShapeDtypeStruct((planes, part, nz), f32),
        ),
        in_specs=[hbm] * 5 + [vmem] * 5,
        out_specs=(hbm, vmem, vmem),
        scratch_shapes=[
            pltpu.VMEM((2, 9, planes, ny, nz), f32),
            pltpu.VMEM((3, planes, ny, nz), f32),
            pltpu.VMEM((2, 3, ny, nz), f32),
            pltpu.VMEM((2, ny, nz), f32),
            pltpu.VMEM((steps, 2, 2, ny, nz), f32),
            pltpu.VMEM((steps, 2, 2, 2, ny, nz), f32),
            pltpu.VMEM((steps, 2, 2, ny, nz), f32),
            pltpu.VMEM((steps, 2, 2, 2, ny, nz), f32),
            pltpu.VMEM((MSG, nrec), f32),
            pltpu.VMEM((n_slab, MSG, nrec), f32),
            pltpu.VMEM((steps, planes * ny, nz), f32),
            pltpu.VMEM((planes * ny, nz), f32),
            pltpu.VMEM((steps, 8, nz), f32),
            pltpu.VMEM((2, planes, ny, nz), f32),
            pltpu.VMEM((n_shot, 2, planes, part, nz), f32),
            dma((5,)),
            dma((5,)),
            dma((10,)),
            dma((10,)),
            dma((steps, 2)),
            dma((steps, 2)),
            dma((steps, 2)),
            dma((steps, 2)),
            dma((n_slab,)),
            dma((n_slab,)),
            dma((n_shot,)),
            dma((n_shot,)),
            dma,
            dma,
        ],
        compiler_params=pltpu.CompilerParams(
            has_side_effects=True, vmem_limit_bytes=24 * 1024 * 1024
        ),
        cost_estimate=pl.CostEstimate(flops=10**7, bytes_accessed=10**6, transcendentals=0),
    )(
        lam,
        mu,
        buo,
        fwd,
        adj,
        wavelet,
        source.reshape(1, 1),
        traces,
        rslab.reshape(1, nrec),
        rcell.reshape(1, nrec),
    )


def solution(mesh):
    in_specs = (
        P("slab", None, None),
        P("slab", None, None),
        P("slab", None, None),
        P("shot", None, "slab", None, None),
        P("shot", None, "slab", None, None),
        P("shot", None),
        P("shot"),
        P("shot", None, "slab"),
        P("slab", None),
        P("slab"),
    )
    out_specs = (
        P("shot", None, "slab", None, None),
        P("slab", "shot", None),
        P("slab", "shot", None),
    )
    body = functools.partial(shards, mesh.shape["shot"], mesh.shape["slab"])
    return jax.shard_map(body, mesh=mesh, in_specs=in_specs, out_specs=out_specs, check_vma=False)
```

time: 302 us -> 58.4 us (0.19); the launches traced: 297 us -> 57.8 us
  starting transfers between devices: 92 us -> 0 us
  waiting for transfers between devices: 81.2 us -> 0 us
  Pallas kernels: 0 us -> 49.7 us
  blocking collectives: 37.4 us -> 0 us
  other arithmetic: 35 us -> 0 us
  local copies, waits for them, and re-layouts: 35.6 us -> 6.76 us
  between operations: 16 us -> 1.35 us
    ppermute x32 -> x0, starting transfers between devices: 91.9 us -> none  [from_behind(): lax.ppermute(value, axis, [(source, source + steps) for source in range(i...]
    reduce_scatter x2 -> x0, waiting for transfers between devices: 59.6 us -> none  [the longest x1 37.1 us: shards(): lax.psum_scatter(grad_lambda, 'shot', scatter_dimension=1, tiled=True)]
    pallas_call x0 -> x1, Pallas kernels: none -> 49.7 us  [shards(): pl.pallas_call(functools.partial(kernel, n_shot, n_slab, steps), out_shap...]
    all_gather x2 -> x0, blocking collectives: 37.4 us -> none  [the longest x1 24.2 us: shards(): lax.all_gather(traces, 'slab', axis=1, tiled=True)]
    slice x60 -> x0, local copies, waits for them, and re-layouts: 35.2 us -> none  [the longest x1 28.9 us: shards(): receiver_push[step_index]]
    ppermute x32 -> x0, waiting for transfers between devices: 21.6 us -> none  [from_behind(): lax.ppermute(value, axis, [(source, source + steps) for source in range(i...]
    scatter-add x2 -> x0, other arithmetic: 9.39 us -> none  [the longest x1 9.37 us: shards(): jnp.zeros((steps_total, cell_count), jnp.float32).at[:, cell_index]]
    mul x12 -> x0, other arithmetic: 8.03 us -> none  [the longest x5 5.09 us: shards(): source_spot * source_wavelet[0, step_index]]
  transfers between devices with their start and end apart: 34 -> 0, of which waited for: 14 -> 0; matrix products, arithmetic and copies ran while one was open for 22% -> 0% of each run, Pallas kernels for 0% -> 0%
where the time goes in v1:
time: 58.4 us; the launch traced here: 57.8 us
  Pallas kernels  49.7 us (85%)
  local copies, waits for them, and re-layouts  6.76 us (12%)
  between operations  1.35 us (2%)
    pallas_call x1, Pallas kernels, shards(): pl.pallas_call(functools.partial(kernel, n_shot, n_slab, steps), out_shap...  49.7 us
    unnamed x21, local copies, waits for them, and re-layouts  6.76 us

profile of v1, /device:TPU:11, one launch (start us, length us, event | category | flops | bytes accessed | tf_op | source)
XLA Modules:
  0.0 57.8 jit_solution(17119207057156722158)
XLA Ops:
  0.6 0.0 copy-start.5
  1.3 0.0 copy-start.6
  1.3 0.0 copy-start.7
  1.3 0.0 copy-start.8
  1.3 0.0 copy-done.5
  1.3 0.6 %copy-done.6 = f32[1,8]{1,0:T(1,128)S(1)} copy-done((f32[1,8]{1,0:T(1,128)S(1)}, f32[1,8]{1,0:T(1,128)}, u32[]{:S(2)}) %copy-start.6) | copy-done | bytes 56
  2.0 0.0 copy-done.7
  2.0 0.0 copy-done.8
  2.0 0.0 copy-start
  2.0 1.0 %copy-done = f32[1,9,2,32,128]{4,3,2,1,0:T(8,128)S(1)} copy-done((f32[1,9,2,32,128]{4,3,2,1,0:T(8,128)S(1)}, f32[1,9,2,32,128]{4,3,2,1,0:T(8,128)}, u32[]{:S(2)}) %copy-start) | copy-done | bytes 294936
  3.0 0.0 copy-start.1
  3.0 1.0 %copy-done.1 = f32[1,9,2,32,128]{4,3,2,1,0:T(8,128)S(1)} copy-done((f32[1,9,2,32,128]{4,3,2,1,0:T(8,128)S(1)}, f32[1,9,2,32,128]{4,3,2,1,0:T(8,128)}, u32[]{:S(2)}) %copy-start.1) | copy-done | bytes 294936
  3.9 0.0 copy-start.2
  3.9 0.8 %copy-done.2 = f32[2,32,128]{2,1,0:T(8,128)S(1)} copy-done((f32[2,32,128]{2,1,0:T(8,128)S(1)}, f32[2,32,128]{2,1,0:T(8,128)}, u32[]{:S(2)}) %copy-start.2) | copy-done | bytes 32792
  4.7 0.0 copy-start.3
  4.7 0.8 %copy-done.3 = f32[2,32,128]{2,1,0:T(8,128)S(1)} copy-done((f32[2,32,128]{2,1,0:T(8,128)S(1)}, f32[2,32,128]{2,1,0:T(8,128)}, u32[]{:S(2)}) %copy-start.3) | copy-done | bytes 32792
  5.4 0.0 copy-start.4
  5.4 0.8 %copy-done.4 = f32[2,32,128]{2,1,0:T(8,128)S(1)} copy-done((f32[2,32,128]{2,1,0:T(8,128)S(1)}, f32[2,32,128]{2,1,0:T(8,128)}, u32[]{:S(2)}) %copy-start.4) | copy-done | bytes 32792
  6.2 49.7 %shard_map.121 = (f32[1,9,2,32,128]{4,3,2,1,0:T(8,128)S(1)}, f32[2,8,128]{2,1,0:T(8,128)S(1)}, f32[2,8,128]{2,1,0:T(8,128)S(1)}) custom-call(f32[2,32,128]{2,1,0:T(8,128)S(1)} %copy-done.2, f32[2,32,128]{2,1,0:T(8,128)S(1)} %copy-done.3, f32[2,32,128]{2,1,0:T(8,128)S(1)} %copy-done.4, f32[1,9,2,32,128]{4,3,2,1,0:T(8,128)S(1)} %copy-done, ...), custom_call_target="tpu_custom_call" | custom-call | flops 10000000 | bytes 1000000 | tf_op jit(solution)/shard_map/pallas_call | solution.py:465
  55.9 0.7 %copy.17 = f32[1,9,2,32,128]{4,3,2,1,0:T(8,128)} copy(f32[1,9,2,32,128]{4,3,2,1,0:T(8,128)S(1)} %get-tuple-element.6) | data formatting | bytes 589824
  56.6 0.6 %copy.18 = f32[2,8,128]{2,1,0:T(8,128)} copy(f32[2,8,128]{2,1,0:T(8,128)S(1)} %get-tuple-element.7) | data formatting | bytes 16384
  57.2 0.6 %copy.19 = f32[2,8,128]{2,1,0:T(8,128)} copy(f32[2,8,128]{2,1,0:T(8,128)S(1)} %get-tuple-element.8) | data formatting | bytes 16384
Async XLA Ops:
  0.6 0.7 %copy-start.5 = (f32[1,8,128]{2,1,0:T(8,128)S(1)}, f32[1,8,128]{2,1,0:T(8,128)}, u32[]{:S(2)}) copy-start(f32[1,8,128]{2,1,0:T(8,128)} %traces_ref.1) | copy-start | bytes 12292
  1.3 0.7 %copy-start.6 = (f32[1,8]{1,0:T(1,128)S(1)}, f32[1,8]{1,0:T(1,128)}, u32[]{:S(2)}) copy-start(f32[1,8]{1,0:T(1,128)} %wavelet_ref.1) | copy-start | bytes 100
  1.3 0.7 %copy-start.7 = (s32[128,1]{0,1:T(1,128)S(1)}, s32[128,1]{0,1:T(1,128)}, u32[]{:S(2)}) copy-start(s32[128,1]{0,1:T(1,128)} %param.18) | copy-start | bytes 1540
  1.3 0.7 %copy-start.8 = (s32[128]{0:T(128)S(1)}, s32[128]{0:T(128)}, u32[]{:S(2)}) copy-start(s32[128]{0:T(128)} %param.19) | copy-start | bytes 1540
  2.0 1.0 %copy-start = (f32[1,9,2,32,128]{4,3,2,1,0:T(8,128)S(1)}, f32[1,9,2,32,128]{4,3,2,1,0:T(8,128)}, u32[]{:S(2)}) copy-start(f32[1,9,2,32,128]{4,3,2,1,0:T(8,128)} %fwd_hbm.1) | copy-start | bytes 884740
  3.0 1.0 %copy-start.1 = (f32[1,9,2,32,128]{4,3,2,1,0:T(8,128)S(1)}, f32[1,9,2,32,128]{4,3,2,1,0:T(8,128)}, u32[]{:S(2)}) copy-start(f32[1,9,2,32,128]{4,3,2,1,0:T(8,128)} %adj_hbm.1) | copy-start | bytes 884740
  3.9 0.8 %copy-start.2 = (f32[2,32,128]{2,1,0:T(8,128)S(1)}, f32[2,32,128]{2,1,0:T(8,128)}, u32[]{:S(2)}) copy-start(f32[2,32,128]{2,1,0:T(8,128)} %lam_hbm.1) | copy-start | bytes 98308
  4.7 0.8 %copy-start.3 = (f32[2,32,128]{2,1,0:T(8,128)S(1)}, f32[2,32,128]{2,1,0:T(8,128)}, u32[]{:S(2)}) copy-start(f32[2,32,128]{2,1,0:T(8,128)} %mu_hbm.1) | copy-start | bytes 98308
  5.4 0.8 %copy-start.4 = (f32[2,32,128]{2,1,0:T(8,128)S(1)}, f32[2,32,128]{2,1,0:T(8,128)}, u32[]{:S(2)}) copy-start(f32[2,32,128]{2,1,0:T(8,128)} %buo_hbm.1) | copy-start | bytes 98308

commit v2 on v1

--- a/solution.py
+++ b/solution.py
@@ -25,14 +25,20 @@
     buo_hbm,
     fwd_hbm,
     adj_hbm,
+    wavelet_hbm,
+    source_hbm,
+    traces_hbm,
+    rslab_hbm,
+    rcell_hbm,
+    adj_out,
+    lam_out,
+    mu_out,
     wavelet_ref,
     source_ref,
     traces_ref,
     rslab_ref,
     rcell_ref,
-    adj_out,
-    lam_out,
-    mu_out,
+    small_sem,
     st,
     par,
     edge,
@@ -80,12 +86,30 @@
             src_ref=src, dst_ref=dst, send_sem=ssem, recv_sem=rsem, device_id=dev, device_id_type=MESH
         )
 
+    small = [
+        pltpu.make_async_copy(a, b, small_sem.at[i])
+        for i, (a, b) in enumerate(
+            (
+                (wavelet_hbm, wavelet_ref),
+                (source_hbm, source_ref),
+                (traces_hbm, traces_ref),
+                (rslab_hbm, rslab_ref),
+                (rcell_hbm, rcell_ref),
+            )
+        )
+    ]
+    for copy in small:
+        copy.start()
     msg[...] = jnp.zeros_like(msg)
+    for copy in small:
+        copy.wait()
     msg[0:steps] = traces_ref[0]
     msg[steps : steps + 1] = rslab_ref[...].astype(jnp.float32)
     msg[steps + 1 : steps + 2] = rcell_ref[...].astype(jnp.float32)
     msg[steps + 2 : steps + 3, 0:steps] = wavelet_ref[...]
-    msg[steps + 3 : steps + 4] = jnp.broadcast_to(source_ref[...].astype(jnp.float32), (1, 128))
+    msg[steps + 3 : steps + 4] = jnp.full((1, msg.shape[1]), source_ref[0], jnp.int32).astype(
+        jnp.float32
+    )
 
     def msg_copy(t):
         return remote(msg, rx_msg.at[slab], msg_send.at[t], msg_recv.at[slab], at_virtual(shot, t))
@@ -168,37 +192,50 @@
     grad[...] = jnp.zeros_like(grad)
     push[...] = jnp.zeros_like(push)
 
-    row_of = lax.broadcasted_iota(jnp.int32, (rows, 128), 0)
-    col_of = lax.broadcasted_iota(jnp.int32, (nz, 128), 0)
-
-    def scatter(q, carry):
-        from_dev = at_virtual(my_shot, q)
-        pltpu.make_async_copy(msg, rx_msg.at[q], msg_recv.at[q]).wait()
-        block = rx_msg[q]
-        named = block[steps : steps + 1].astype(jnp.int32)
-        cell = block[steps + 1 : steps + 2].astype(jnp.int32)
-        row = jnp.where(named == my_slab, cell // nz, -1)
-        hit = row_of == row
-        column = (col_of == lax.rem(cell, nz)).astype(jnp.float32).astype(jnp.bfloat16)
-        trace = block[0:steps]
-        high = trace.astype(jnp.bfloat16).astype(jnp.float32)
-        middle = (trace - high).astype(jnp.bfloat16).astype(jnp.float32)
-        low = trace - high - middle
+    nrec = msg.shape[1]
+    row_of = lax.broadcasted_iota(jnp.int32, (rows, nrec), 0)
+    col_of = lax.broadcasted_iota(jnp.int32, (nz, nrec), 0)
+
+    def scatter(pair, carry):
+        left, right = [], []
+        for q in (2 * pair, 2 * pair + 1):
+            pltpu.make_async_copy(msg, rx_msg.at[q], msg_recv.at[q]).wait()
+            block = rx_msg[q]
+            named = block[steps : steps + 1].astype(jnp.int32)
+            cell = block[steps + 1 : steps + 2].astype(jnp.int32)
+            row = jnp.where(named == my_slab, cell // nz, -1)
+            hit = row_of == row
+            column = (col_of == lax.rem(cell, nz)).astype(jnp.float32).astype(jnp.bfloat16)
+            trace = block[0:steps]
+            high = trace.astype(jnp.bfloat16).astype(jnp.float32)
+            low = trace - high
+            left.append(
+                jnp.concatenate(
+                    [
+                        jnp.where(hit, term[k : k + 1], 0.0).astype(jnp.bfloat16)
+                        for term in (high, low)
+                        for k in range(steps)
+                    ],
+                    axis=0,
+                )
+            )
+            right.append(column)
+        out = lax.dot_general(
+            jnp.concatenate(left, axis=1),
+            jnp.concatenate(right, axis=1),
+            (((1,), (1,)), ((), ())),
+            preferred_element_type=jnp.float32,
+        )
         for k in range(steps):
-            left = jnp.concatenate(
-                [jnp.where(hit, part[k : k + 1], 0.0) for part in (high, middle, low)], axis=0
-            ).astype(jnp.bfloat16)
-            out = lax.dot_general(
-                left, column, (((1,), (1,)), ((), ())), preferred_element_type=jnp.float32
-            )
-            push[k] += out[0:rows] + out[rows : 2 * rows] + out[2 * rows :]
+            push[k] += out[k * rows : (k + 1) * rows] + out[(steps + k) * rows : (steps + k + 1) * rows]
         return carry
 
-    lax.fori_loop(0, n_slab, scatter, 0)
+    lax.fori_loop(0, n_slab // 2, scatter, 0)
 
     head = rx_msg[my_slab]
     source = head[steps + 3 : steps + 4].astype(jnp.int32) - my_slab * cells
-    flat = row_of * nz + lax.broadcasted_iota(jnp.int32, (rows, nz), 1)
+    flat = lax.broadcasted_iota(jnp.int32, (rows, nz), 0) * nz
+    flat = flat + lax.broadcasted_iota(jnp.int32, (rows, nz), 1)
     spot[...] = (flat == source).astype(jnp.float32)
     for k in range(steps):
         amp[k] = jnp.broadcast_to(DT * head[steps + 2 : steps + 3, k : k + 1], (8, nz))
@@ -254,6 +291,20 @@
             remote(tx_s.at[k, 0], rx_s.at[k, 1], s_send.at[k, 0], s_recv.at[k, 1], prev_dev),
             remote(tx_s.at[k, 1], rx_s.at[k, 0], s_send.at[k, 1], s_recv.at[k, 0], next_dev),
         )
+
+    groups = ((0, 3), (3, 6), (8, 9), (6, 8))
+
+    def home_local(n):
+        a, b = groups[n]
+        return pltpu.make_async_copy(st.at[1, a:b], adj_out.at[0, a:b], out_recv.at[n])
+
+    def home_away(n):
+        a, b = groups[n]
+        return remote(st.at[1, a:b], adj_out.at[0, a:b], out_send.at[n], out_recv.at[n], partner)
+
+    def go_home(n):
+        pl.when(stays)(lambda: home_local(n).start())
+        pl.when(moves)(lambda: home_away(n).start())
 
     def step(k, carry):
         for w in range(2):
@@ -292,6 +343,8 @@
                     edge[w, 0] = edge[w, 0] - change
                 else:
                     st[w, 0, i - 1] = st[w, 0, i - 1] - change
+
+        pl.when(k == steps - 1)(lambda: go_home(0))
 
         for i in range(2):
             terms = []
@@ -327,6 +380,8 @@
             pl.when(has_prev)(lambda: s_back.start())
             pl.when(has_next)(lambda: s_ahead.start())
 
+        pl.when(k == steps - 1)(lambda: go_home(1))
+
         for i in range(2):
             eyz = []
             for w in range(2):
@@ -335,6 +390,8 @@
                 st[w, 8, i] = st[w, 8, i] - par[1, i] * strain
                 eyz.append(strain)
             grad[1, i] += eyz[0] * eyz[1]
+
+        pl.when(k == steps - 1)(lambda: go_home(2))
 
         pl.when(has_prev)(lambda: ahead.wait_recv())
         pl.when(has_next)(lambda: back.wait_recv())
@@ -361,9 +418,7 @@
 
     lax.fori_loop(0, steps, step, 0)
 
-    out_local = pltpu.make_async_copy(st.at[1], adj_out.at[0], out_recv)
-    out_remote = remote(st.at[1], adj_out.at[0], out_send, out_recv, partner)
-
+    go_home(3)
     grad[...] = DT * grad[...]
     part = ny // n_shot
 
@@ -386,9 +441,6 @@
         @pl.when(own)
         def _(t=t):
             rx_grad[t] = grad[:, :, t * part : (t + 1) * part]
-
-    pl.when(stays)(lambda: out_local.start())
-    pl.when(moves)(lambda: out_remote.start())
 
     for t in range(n_shot):
         own = jnp.logical_and(stays, t == shot)
@@ -444,13 +496,28 @@
         for copy in prev_copies:
             copy.wait_send()
 
-    pl.when(stays)(lambda: out_local.wait())
+    @pl.when(stays)
+    def _():
+        for n in range(len(groups)):
+            home_local(n).wait()
 
     @pl.when(moves)
     def _():
         for copy in swap_in:
             copy.wait_send()
-        out_remote.wait()
+        for n in range(len(groups)):
+            home_away(n).wait()
+
+
+def deliver(a, b, c, a_out, b_out, c_out, sem):
+    copies = [
+        pltpu.make_async_copy(src, dst, sem.at[i])
+        for i, (src, dst) in enumerate(((a, a_out), (b, b_out), (c, c_out)))
+    ]
+    for copy in copies:
+        copy.start()
+    for copy in copies:
+        copy.wait()
 
 
 def shards(n_shot, n_slab, lam, mu, buo, fwd, adj, wavelet, source, traces, rslab, rcell):
@@ -462,16 +529,22 @@
     hbm = pl.BlockSpec(memory_space=pl.ANY)
     dma = pltpu.SemaphoreType.DMA
     part = ny // n_shot
-    return pl.pallas_call(
+    outs = pl.pallas_call(
         functools.partial(kernel, n_shot, n_slab, steps),
         out_shape=(
             jax.ShapeDtypeStruct((1, 9, planes, ny, nz), f32),
             jax.ShapeDtypeStruct((planes, part, nz), f32),
             jax.ShapeDtypeStruct((planes, part, nz), f32),
         ),
-        in_specs=[hbm] * 5 + [vmem] * 5,
+        in_specs=[hbm] * 10,
         out_specs=(hbm, vmem, vmem),
         scratch_shapes=[
+            pltpu.VMEM((1, steps), f32),
+            pltpu.SMEM((1,), jnp.int32),
+            pltpu.VMEM((1, steps, nrec), f32),
+            pltpu.VMEM((1, nrec), jnp.int32),
+            pltpu.VMEM((1, nrec), jnp.int32),
+            dma((5,)),
             pltpu.VMEM((2, 9, planes, ny, nz), f32),
             pltpu.VMEM((3, planes, ny, nz), f32),
             pltpu.VMEM((2, 3, ny, nz), f32),
@@ -499,11 +572,11 @@
             dma((n_slab,)),
             dma((n_shot,)),
             dma((n_shot,)),
-            dma,
-            dma,
+            dma((4,)),
+            dma((4,)),
         ],
         compiler_params=pltpu.CompilerParams(
-            has_side_effects=True, vmem_limit_bytes=24 * 1024 * 1024
+            has_side_effects=True, vmem_limit_bytes=60 * 1024 * 1024
         ),
         cost_estimate=pl.CostEstimate(flops=10**7, bytes_accessed=10**6, transcendentals=0),
     )(
@@ -513,11 +586,20 @@
         fwd,
         adj,
         wavelet,
-        source.reshape(1, 1),
+        source,
         traces,
         rslab.reshape(1, nrec),
         rcell.reshape(1, nrec),
     )
+    return pl.pallas_call(
+        deliver,
+        out_shape=tuple(jax.ShapeDtypeStruct(o.shape, o.dtype) for o in outs),
+        in_specs=[hbm] * 3,
+        out_specs=(hbm,) * 3,
+        scratch_shapes=[dma((3,))],
+        compiler_params=pltpu.CompilerParams(vmem_limit_bytes=60 * 1024 * 1024),
+        cost_estimate=pl.CostEstimate(flops=0, bytes_accessed=10**6, transcendentals=0),
+    )(*outs)
 
 
 def solution(mesh):

time: 58.4 us -> 61.6 us (1.055)
  Pallas kernels: 49.7 us -> 60.1 us
  local copies, waits for them, and re-layouts: 6.76 us -> 0 us
    pallas_call x0 -> x1, Pallas kernels: none -> 10.6 us  [shards(): pl.pallas_call(deliver, out_shape=tuple((jax.ShapeDtypeStruct(o.shape, o....]
    unnamed x21 -> x0, local copies, waits for them, and re-layouts: 6.76 us -> none
where the time goes in v2:
time: 61.6 us; the launch traced here: 61.4 us
  Pallas kernels  60.1 us (98%)
  between operations  1.29 us (2%)
    pallas_call x1, Pallas kernels, shards(): pl.pallas_call(functools.partial(kernel, n_shot, n_slab, steps), out_shap...  49.5 us
    pallas_call x1, Pallas kernels, shards(): pl.pallas_call(deliver, out_shape=tuple((jax.ShapeDtypeStruct(o.shape, o....  10.6 us

profile of v2, /device:TPU:11, one launch (start us, length us, event | category | flops | bytes accessed | tf_op | source)
XLA Modules:
  0.0 61.4 jit_solution(15372845603034196776)
XLA Ops:
  1.3 49.5 %shard_map.121 = (f32[1,9,2,32,128]{4,3,2,1,0:T(8,128)}, f32[2,8,128]{2,1,0:T(8,128)}, f32[2,8,128]{2,1,0:T(8,128)}) custom-call(f32[2,32,128]{2,1,0:T(8,128)} %lam_hbm.1, f32[2,32,128]{2,1,0:T(8,128)} %mu_hbm.1, f32[2,32,128]{2,1,0:T(8,128)} %buo_hbm.1, f32[1,9,2,32,128]{4,3,2,1,0:T(8,128)} %fwd_hbm.1, f32[1,9,2,32,128]{4,3,2,1,0:T(8,128)} %adj_hbm.1, ...), custom_call_target="tpu_custom_call" | custom-call | flops 10000000 | bytes 1000000 | tf_op jit(solution)/shard_map/pallas_call | solution.py:532
  50.8 10.6 %shard_map.122 = (f32[1,9,2,32,128]{4,3,2,1,0:T(8,128)}, f32[2,8,128]{2,1,0:T(8,128)}, f32[2,8,128]{2,1,0:T(8,128)}) custom-call(f32[1,9,2,32,128]{4,3,2,1,0:T(8,128)} %get-tuple-element.6.a, f32[2,8,128]{2,1,0:T(8,128)} %get-tuple-element.7.b, f32[2,8,128]{2,1,0:T(8,128)} %get-tuple-element.8.c), custom_call_target="tpu_custom_call" | custom-call | bytes 1000000 | tf_op jit(solution)/shard_map/pallas_call | solution.py:594

commit v3 on v2

--- a/solution.py
+++ b/solution.py
@@ -54,6 +54,12 @@
     amp,
     grad,
     rx_grad,
+    own,
+    own_par,
+    home,
+    own_sem,
+    swap_recv,
+    home_sem,
     in_send,
     in_recv,
     edge_send,
@@ -100,6 +106,59 @@
     ]
     for copy in small:
         copy.start()
+    own_pairs = [
+        (fwd_hbm.at[0], own.at[0]),
+        (adj_hbm.at[0], own.at[1]),
+        (lam_hbm, own_par.at[0]),
+        (mu_hbm, own_par.at[1]),
+        (buo_hbm, own_par.at[2]),
+    ]
+    own_in = [pltpu.make_async_copy(a, b, own_sem.at[i]) for i, (a, b) in enumerate(own_pairs)]
+    for copy in own_in:
+        copy.start()
+    work_pairs = [
+        (fwd_hbm.at[0], st.at[0]),
+        (adj_hbm.at[0], st.at[1]),
+        (lam_hbm, par.at[0]),
+        (mu_hbm, par.at[1]),
+        (buo_hbm, par.at[2]),
+    ]
+    local_in = [pltpu.make_async_copy(a, b, in_recv.at[i]) for i, (a, b) in enumerate(work_pairs)]
+
+    @pl.when(stays)
+    def _():
+        for copy in local_in:
+            copy.start()
+
+    first_shot, first_slab = shot - lax.rem(shot, 2), slab - lax.rem(slab, 2)
+    barrier = pltpu.get_barrier_semaphore()
+
+    def greet(q, carry):
+        for core in range(2):
+            me = jnp.logical_and(q == slab, first_shot + core == shot)
+
+            @pl.when(jnp.logical_not(me))
+            def _(core=core):
+                pl.semaphore_signal(
+                    barrier, inc=1, device_id=(first_shot + core, q), device_id_type=MESH
+                )
+
+        return carry
+
+    lax.fori_loop(0, n_slab, greet, 0)
+    for other in range(0, n_shot, 2):
+
+        @pl.when(first_shot != other)
+        def _(other=other):
+            for t in (other, other + 1):
+                for half in range(2):
+                    pl.semaphore_signal(
+                        barrier,
+                        inc=1,
+                        device_id=(jnp.int32(t), first_slab + half),
+                        device_id_type=MESH,
+                    )
+
     msg[...] = jnp.zeros_like(msg)
     for copy in small:
         copy.wait()
@@ -111,6 +170,8 @@
         jnp.float32
     )
 
+    pl.semaphore_wait(barrier, 2 * n_slab - 1 + 2 * (n_shot - 2))
+
     def msg_copy(t):
         return remote(msg, rx_msg.at[slab], msg_send.at[t], msg_recv.at[slab], at_virtual(shot, t))
 
@@ -130,14 +191,14 @@
     orig_prev = at_virtual(shot, jnp.maximum(slab - 1, 0))
     orig_next = at_virtual(shot, jnp.minimum(slab + 1, n_slab - 1))
     to_next, to_prev = [], []
-    for w, field in enumerate((fwd_hbm, adj_hbm)):
+    for w in range(2):
         to_next += [
-            (field.at[0, 0, 1], edge.at[w, 0]),
-            (field.at[0, 6:8, 1], edge.at[w, 1:3]),
-            (field.at[0, 3, 1], rx_s.at[0, 0, w]),
+            (own.at[w, 0, 1], edge.at[w, 0]),
+            (own.at[w, 6:8, 1], edge.at[w, 1:3]),
+            (own.at[w, 3, 1], rx_s.at[0, 0, w]),
         ]
-        to_prev += [(field.at[0, 3, 0], rx_s.at[0, 1, w])]
-    to_next += [(mu_hbm.at[1], edge_par.at[0]), (buo_hbm.at[1], edge_par.at[1])]
+        to_prev += [(own.at[w, 3, 0], rx_s.at[0, 1, w])]
+    to_next += [(own_par.at[1, 1], edge_par.at[0]), (own_par.at[2, 1], edge_par.at[1])]
     next_copies = [
         remote(a, b, edge_send.at[i], edge_recv.at[i], orig_next) for i, (a, b) in enumerate(to_next)
     ]
@@ -146,6 +207,8 @@
         for i, (a, b) in enumerate(to_prev)
     ]
     sends_next, sends_prev = slab < n_slab - 1, slab > 0
+    for copy in own_in:
+        copy.wait()
 
     @pl.when(sends_next)
     def _():
@@ -157,20 +220,11 @@
         for copy in prev_copies:
             copy.start()
 
-    pairs = [
-        (fwd_hbm.at[0], st.at[0]),
-        (adj_hbm.at[0], st.at[1]),
-        (lam_hbm, par.at[0]),
-        (mu_hbm, par.at[1]),
-        (buo_hbm, par.at[2]),
+    swap_pairs = [(own.at[w, a : a + 3], st.at[w, a : a + 3]) for a in (0, 3, 6) for w in range(2)]
+    swap_pairs += [(own_par, par)]
+    swap_in = [
+        remote(a, b, in_send.at[i], swap_recv.at[i], partner) for i, (a, b) in enumerate(swap_pairs)
     ]
-    local_in = [pltpu.make_async_copy(a, b, in_recv.at[i]) for i, (a, b) in enumerate(pairs)]
-    swap_in = [remote(a, b, in_send.at[i], in_recv.at[i], partner) for i, (a, b) in enumerate(pairs)]
-
-    @pl.when(stays)
-    def _():
-        for copy in local_in:
-            copy.start()
 
     @pl.when(moves)
     def _():
@@ -296,11 +350,15 @@
 
     def home_local(n):
         a, b = groups[n]
-        return pltpu.make_async_copy(st.at[1, a:b], adj_out.at[0, a:b], out_recv.at[n])
+        return pltpu.make_async_copy(st.at[1, a:b], adj_out.at[0, a:b], home_sem.at[n])
+
+    def home_land(n):
+        a, b = groups[n]
+        return pltpu.make_async_copy(home.at[a:b], adj_out.at[0, a:b], home_sem.at[n])
 
     def home_away(n):
         a, b = groups[n]
-        return remote(st.at[1, a:b], adj_out.at[0, a:b], out_send.at[n], out_recv.at[n], partner)
+        return remote(st.at[1, a:b], home.at[a:b], out_send.at[n], out_recv.at[n], partner)
 
     def go_home(n):
         pl.when(stays)(lambda: home_local(n).start())
@@ -455,6 +513,12 @@
                 (jnp.int32(t), my_slab),
             ).wait_recv()
 
+    @pl.when(moves)
+    def _():
+        for n in range(len(groups)):
+            home_away(n).wait_recv()
+            home_land(n).start()
+
     total = rx_grad[0]
     for t in range(1, n_shot):
         total = total + rx_grad[t]
@@ -506,17 +570,20 @@
         for copy in swap_in:
             copy.wait_send()
         for n in range(len(groups)):
-            home_away(n).wait()
-
-
-def deliver(a, b, c, a_out, b_out, c_out, sem):
-    copies = [
-        pltpu.make_async_copy(src, dst, sem.at[i])
-        for i, (src, dst) in enumerate(((a, a_out), (b, b_out), (c, c_out)))
-    ]
-    for copy in copies:
+            home_away(n).wait_send()
+            home_land(n).wait()
+
+
+def deliver(a, b, c, a_out, b_out, c_out, a_mid, b_mid, c_mid, sem):
+    pairs = ((a, a_mid, a_out), (b, b_mid, b_out), (c, c_mid, c_out))
+    loads = [pltpu.make_async_copy(src, mid, sem.at[0, i]) for i, (src, mid, _) in enumerate(pairs)]
+    stores = [pltpu.make_async_copy(mid, dst, sem.at[1, i]) for i, (_, mid, dst) in enumerate(pairs)]
+    for copy in loads:
         copy.start()
-    for copy in copies:
+    for load, store in zip(loads, stores):
+        load.wait()
+        store.start()
+    for copy in stores:
         copy.wait()
 
 
@@ -560,7 +627,13 @@
             pltpu.VMEM((steps, 8, nz), f32),
             pltpu.VMEM((2, planes, ny, nz), f32),
             pltpu.VMEM((n_shot, 2, planes, part, nz), f32),
+            pltpu.VMEM((2, 9, planes, ny, nz), f32),
+            pltpu.VMEM((3, planes, ny, nz), f32),
+            pltpu.VMEM((9, planes, ny, nz), f32),
             dma((5,)),
+            dma((7,)),
+            dma((4,)),
+            dma((7,)),
             dma((5,)),
             dma((10,)),
             dma((10,)),
@@ -576,7 +649,7 @@
             dma((4,)),
         ],
         compiler_params=pltpu.CompilerParams(
-            has_side_effects=True, vmem_limit_bytes=60 * 1024 * 1024
+            has_side_effects=True, collective_id=0, vmem_limit_bytes=60 * 1024 * 1024
         ),
         cost_estimate=pl.CostEstimate(flops=10**7, bytes_accessed=10**6, transcendentals=0),
     )(
@@ -596,7 +669,7 @@
         out_shape=tuple(jax.ShapeDtypeStruct(o.shape, o.dtype) for o in outs),
         in_specs=[hbm] * 3,
         out_specs=(hbm,) * 3,
-        scratch_shapes=[dma((3,))],
+        scratch_shapes=[pltpu.VMEM(o.shape, o.dtype) for o in outs] + [dma((2, 3))],
         compiler_params=pltpu.CompilerParams(vmem_limit_bytes=60 * 1024 * 1024),
         cost_estimate=pl.CostEstimate(flops=0, bytes_accessed=10**6, transcendentals=0),
     )(*outs)

time: 61.6 us -> 50.3 us (0.82)
  Pallas kernels: 60.1 us -> 48.8 us
    pallas_call x1, Pallas kernels: 10.6 us -> 1.73 us  [shards(): pl.pallas_call(deliver, out_shape=tuple((jax.ShapeDtypeStruct(o.shape, o....]
    pallas_call x1, Pallas kernels: 49.5 us -> 47.1 us  [shards(): pl.pallas_call(functools.partial(kernel, n_shot, n_slab, steps), out_shap...]
where the time goes in v3:
time: 50.3 us; the launch traced here: 50.1 us
  Pallas kernels  48.8 us (97%)
  between operations  1.29 us (3%)
    pallas_call x1, Pallas kernels, shards(): pl.pallas_call(functools.partial(kernel, n_shot, n_slab, steps), out_shap...  47.1 us
    pallas_call x1, Pallas kernels, shards(): pl.pallas_call(deliver, out_shape=tuple((jax.ShapeDtypeStruct(o.shape, o....  1.73 us

profile of v3, /device:TPU:11, one launch (start us, length us, event | category | flops | bytes accessed | tf_op | source)
XLA Modules:
  0.0 50.1 jit_solution(7566006354355363860)
XLA Ops:
  1.3 47.1 %shard_map.121 = (f32[1,9,2,32,128]{4,3,2,1,0:T(8,128)}, f32[2,8,128]{2,1,0:T(8,128)}, f32[2,8,128]{2,1,0:T(8,128)}) custom-call(f32[2,32,128]{2,1,0:T(8,128)} %lam_hbm.1, f32[2,32,128]{2,1,0:T(8,128)} %mu_hbm.1, f32[2,32,128]{2,1,0:T(8,128)} %buo_hbm.1, f32[1,9,2,32,128]{4,3,2,1,0:T(8,128)} %fwd_hbm.1, f32[1,9,2,32,128]{4,3,2,1,0:T(8,128)} %adj_hbm.1, ...), custom_call_target="tpu_custom_call" | custom-call | flops 10000000 | bytes 1000000 | tf_op jit(solution)/shard_map/pallas_call | solution.py:599
  48.4 1.7 %shard_map.122 = (f32[1,9,2,32,128]{4,3,2,1,0:T(8,128)}, f32[2,8,128]{2,1,0:T(8,128)}, f32[2,8,128]{2,1,0:T(8,128)}) custom-call(f32[1,9,2,32,128]{4,3,2,1,0:T(8,128)} %get-tuple-element.6.a, f32[2,8,128]{2,1,0:T(8,128)} %get-tuple-element.7.b, f32[2,8,128]{2,1,0:T(8,128)} %get-tuple-element.8.c), custom_call_target="tpu_custom_call" | custom-call | bytes 1000000 | tf_op jit(solution)/shard_map/pallas_call | solution.py:667

commit v4 on v3

--- a/solution.py
+++ b/solution.py
@@ -190,46 +190,45 @@
 
     orig_prev = at_virtual(shot, jnp.maximum(slab - 1, 0))
     orig_next = at_virtual(shot, jnp.minimum(slab + 1, n_slab - 1))
-    to_next, to_prev = [], []
-    for w in range(2):
-        to_next += [
+    sends_next, sends_prev = slab < n_slab - 1, slab > 0
+    mat_next = [(own_par.at[1, 1], edge_par.at[0]), (own_par.at[2, 1], edge_par.at[1])]
+    wave_next = [
+        [
+            (own.at[w, 6:8, 1], edge.at[w, 1:3]),
             (own.at[w, 0, 1], edge.at[w, 0]),
-            (own.at[w, 6:8, 1], edge.at[w, 1:3]),
             (own.at[w, 3, 1], rx_s.at[0, 0, w]),
         ]
-        to_prev += [(own.at[w, 3, 0], rx_s.at[0, 1, w])]
-    to_next += [(own_par.at[1, 1], edge_par.at[0]), (own_par.at[2, 1], edge_par.at[1])]
-    next_copies = [
-        remote(a, b, edge_send.at[i], edge_recv.at[i], orig_next) for i, (a, b) in enumerate(to_next)
+        for w in range(2)
     ]
-    prev_copies = [
-        remote(a, b, edge_send.at[8 + i], edge_recv.at[8 + i], orig_prev)
-        for i, (a, b) in enumerate(to_prev)
-    ]
-    sends_next, sends_prev = slab < n_slab - 1, slab > 0
-    for copy in own_in:
+    wave_prev = [[(own.at[w, 3, 0], rx_s.at[0, 1, w])] for w in range(2)]
+    swaps = [[(own.at[w, a : a + 3], st.at[w, a : a + 3]) for a in (6, 3, 0)] for w in range(2)]
+
+    def batch(pairs, ssem, rsem, start, dev):
+        return [
+            remote(a, b, ssem.at[start + n], rsem.at[start + n], dev) for n, (a, b) in enumerate(pairs)
+        ]
+
+    mat_edge = batch(mat_next, edge_send, edge_recv, 0, orig_next)
+    mat_swap = batch([(own_par, par)], in_send, swap_recv, 0, partner)
+    edge_next = [batch(wave_next[w], edge_send, edge_recv, 2 + 4 * w, orig_next) for w in range(2)]
+    edge_prev = [batch(wave_prev[w], edge_send, edge_recv, 5 + 4 * w, orig_prev) for w in range(2)]
+    wave_swap = [batch(swaps[w], in_send, swap_recv, 1 + 3 * w, partner) for w in range(2)]
+
+    def when_all(condition, copies, action):
+        @pl.when(condition)
+        def _():
+            for copy in copies:
+                getattr(copy, action)()
+
+    for copy in own_in[2:]:
         copy.wait()
-
-    @pl.when(sends_next)
-    def _():
-        for copy in next_copies:
-            copy.start()
-
-    @pl.when(sends_prev)
-    def _():
-        for copy in prev_copies:
-            copy.start()
-
-    swap_pairs = [(own.at[w, a : a + 3], st.at[w, a : a + 3]) for a in (0, 3, 6) for w in range(2)]
-    swap_pairs += [(own_par, par)]
-    swap_in = [
-        remote(a, b, in_send.at[i], swap_recv.at[i], partner) for i, (a, b) in enumerate(swap_pairs)
-    ]
-
-    @pl.when(moves)
-    def _():
-        for copy in swap_in:
-            copy.start()
+    when_all(sends_next, mat_edge, "start")
+    when_all(moves, mat_swap, "start")
+    for w in range(2):
+        own_in[w].wait()
+        when_all(sends_next, edge_next[w], "start")
+        when_all(sends_prev, edge_prev[w], "start")
+        when_all(moves, wave_swap[w], "start")
 
     @pl.when(jnp.logical_not(has_prev))
     def _():
@@ -294,25 +293,9 @@
     for k in range(steps):
         amp[k] = jnp.broadcast_to(DT * head[steps + 2 : steps + 3, k : k + 1], (8, nz))
 
-    @pl.when(stays)
-    def _():
-        for copy in local_in:
-            copy.wait()
-
-    @pl.when(moves)
-    def _():
-        for copy in swap_in:
-            copy.wait_recv()
-
-    @pl.when(has_prev)
-    def _():
-        for copy in next_copies:
-            copy.wait_recv()
-
-    @pl.when(has_next)
-    def _():
-        for copy in prev_copies:
-            copy.wait_recv()
+    when_all(stays, local_in[2:], "wait")
+    when_all(moves, mat_swap, "wait_recv")
+    when_all(has_prev, mat_edge, "wait_recv")
 
     y_at = lax.broadcasted_iota(jnp.int32, (ny, nz), 0)
     z_at = lax.broadcasted_iota(jnp.int32, (ny, nz), 1)
@@ -334,16 +317,24 @@
     par[2] = DT * par[2]
     edge_par[...] = DT * edge_par[...]
 
-    def v_copies(k):
-        return (
-            remote(tx_v.at[k, 0], rx_v.at[k, 1], v_send.at[k, 0], v_recv.at[k, 1], prev_dev),
-            remote(tx_v.at[k, 1], rx_v.at[k, 0], v_send.at[k, 1], v_recv.at[k, 0], next_dev),
-        )
-
-    def s_copies(k):
-        return (
-            remote(tx_s.at[k, 0], rx_s.at[k, 1], s_send.at[k, 0], s_recv.at[k, 1], prev_dev),
-            remote(tx_s.at[k, 1], rx_s.at[k, 0], s_send.at[k, 1], s_recv.at[k, 0], next_dev),
+    def v_back(k, w):
+        return remote(
+            tx_v.at[k, 0, w], rx_v.at[k, 1, w], v_send.at[k, 0, w], v_recv.at[k, 1, w], prev_dev
+        )
+
+    def v_ahead(k, w):
+        return remote(
+            tx_v.at[k, 1, w], rx_v.at[k, 0, w], v_send.at[k, 1, w], v_recv.at[k, 0, w], next_dev
+        )
+
+    def s_back(k, w):
+        return remote(
+            tx_s.at[k, 0, w], rx_s.at[k, 1, w], s_send.at[k, 0, w], s_recv.at[k, 1, w], prev_dev
+        )
+
+    def s_ahead(k, w):
+        return remote(
+            tx_s.at[k, 1, w], rx_s.at[k, 0, w], s_send.at[k, 1, w], s_recv.at[k, 0, w], next_dev
         )
 
     groups = ((0, 3), (3, 6), (8, 9), (6, 8))
@@ -364,33 +355,32 @@
         pl.when(stays)(lambda: home_local(n).start())
         pl.when(moves)(lambda: home_away(n).start())
 
+    def transverse(k, w):
+        for i in range(2):
+            sxy0 = edge[w, 1] if i == 0 else st[w, 6, 0]
+            sxz0 = edge[w, 2] if i == 0 else st[w, 7, 0]
+            syy, szz, syz = st[w, 4, i], st[w, 5, i], st[w, 8, i]
+            vy = st[w, 1, i] - par[2, i] * (
+                (st[w, 6, i] - sxy0) + (yn(syy) - syy) + (syz - zp(syz))
+            )
+            vz = st[w, 2, i] - par[2, i] * (
+                (st[w, 7, i] - sxz0) + (syz - yp(syz)) + (zn(szz) - szz)
+            )
+            st[w, 1, i] = vy
+            st[w, 2, i] = vz
+            tx_v[k, i, w, 0] = vy
+            tx_v[k, i, w, 1] = vz
+        pl.when(has_prev)(lambda: v_back(k, w).start())
+        pl.when(has_next)(lambda: v_ahead(k, w).start())
+
     def step(k, carry):
+        normal = []
         for w in range(2):
-            for i in range(2):
-                sxy0 = edge[w, 1] if i == 0 else st[w, 6, 0]
-                sxz0 = edge[w, 2] if i == 0 else st[w, 7, 0]
-                syy, szz, syz = st[w, 4, i], st[w, 5, i], st[w, 8, i]
-                vy = st[w, 1, i] - par[2, i] * (
-                    (st[w, 6, i] - sxy0) + (yn(syy) - syy) + (syz - zp(syz))
-                )
-                vz = st[w, 2, i] - par[2, i] * (
-                    (st[w, 7, i] - sxz0) + (syz - yp(syz)) + (zn(szz) - szz)
-                )
-                st[w, 1, i] = vy
-                st[w, 2, i] = vz
-                tx_v[k, i, w, 0] = vy
-                tx_v[k, i, w, 1] = vz
-        back, ahead = v_copies(k)
-        pl.when(has_prev)(lambda: back.start())
-        pl.when(has_next)(lambda: ahead.start())
-
-        @pl.when(k > 0)
-        def _():
-            s_back, s_ahead = s_copies(k)
-            pl.when(has_prev)(lambda: s_ahead.wait_recv())
-            pl.when(has_next)(lambda: s_back.wait_recv())
-
-        for w in range(2):
+            @pl.when(k > 0)
+            def _(w=w):
+                pl.when(has_prev)(lambda: s_ahead(k, w).wait_recv())
+                pl.when(has_next)(lambda: s_back(k, w).wait_recv())
+
             sxx = [rx_s[k, 0, w], st[w, 3, 0], st[w, 3, 1], rx_s[k, 1, w]]
             for i in range(3):
                 sxy = edge[w, 1] if i == 0 else st[w, 6, i - 1]
@@ -402,60 +392,69 @@
                 else:
                     st[w, 0, i - 1] = st[w, 0, i - 1] - change
 
-        pl.when(k == steps - 1)(lambda: go_home(0))
-
-        for i in range(2):
             terms = []
-            at = pl.ds(i * ny, ny)
-            gains = (amp[k, 0:1] * spot[at], DT * push[k, at])
-            for w in range(2):
+            for i in range(2):
+                at = pl.ds(i * ny, ny)
+                gain = amp[k, 0:1] * spot[at] if w == 0 else DT * push[k, at]
                 vx0 = edge[w, 0] if i == 0 else st[w, 0, 0]
                 vy, vz = st[w, 1, i], st[w, 2, i]
                 exx = st[w, 0, i] - vx0
                 eyy = vy - yp(vy)
                 ezz = vz - zp(vz)
                 tr = exx + eyy + ezz
-                common = par[0, i] * tr + gains[w]
+                common = par[0, i] * tr + gain
                 twice = 2.0 * par[1, i]
-                sxx = st[w, 3, i] - (common + twice * exx)
-                st[w, 3, i] = sxx
-                tx_s[k, i, w] = sxx
+                new = st[w, 3, i] - (common + twice * exx)
+                st[w, 3, i] = new
+                tx_s[k, i, w] = new
                 st[w, 4, i] = st[w, 4, i] - (common + twice * eyy)
                 st[w, 5, i] = st[w, 5, i] - (common + twice * ezz)
                 terms.append((exx, eyy, ezz, tr))
-            f, a = terms
+            normal.append(terms)
+
+            @pl.when(k < steps - 1)
+            def _(w=w):
+                back = remote(
+                    tx_s.at[k, 0, w],
+                    rx_s.at[k + 1, 1, w],
+                    s_send.at[k, 0, w],
+                    s_recv.at[k + 1, 1, w],
+                    prev_dev,
+                )
+                ahead = remote(
+                    tx_s.at[k, 1, w],
+                    rx_s.at[k + 1, 0, w],
+                    s_send.at[k, 1, w],
+                    s_recv.at[k + 1, 0, w],
+                    next_dev,
+                )
+                pl.when(has_prev)(lambda: back.start())
+                pl.when(has_next)(lambda: ahead.start())
+
+        @pl.when(k == steps - 1)
+        def _():
+            go_home(0)
+            go_home(1)
+
+        for i in range(2):
+            f, a = normal[0][i], normal[1][i]
             grad[0, i] += f[3] * a[3]
-            grad[1, i] += 2.0 * (f[0] * a[0] + f[1] * a[1] + f[2] * a[2])
-
-        @pl.when(k < steps - 1)
-        def _():
-            s_back = remote(
-                tx_s.at[k, 0], rx_s.at[k + 1, 1], s_send.at[k, 0], s_recv.at[k + 1, 1], prev_dev
-            )
-            s_ahead = remote(
-                tx_s.at[k, 1], rx_s.at[k + 1, 0], s_send.at[k, 1], s_recv.at[k + 1, 0], next_dev
-            )
-            pl.when(has_prev)(lambda: s_back.start())
-            pl.when(has_next)(lambda: s_ahead.start())
-
-        pl.when(k == steps - 1)(lambda: go_home(1))
-
-        for i in range(2):
             eyz = []
             for w in range(2):
                 vy, vz = st[w, 1, i], st[w, 2, i]
                 strain = (zn(vy) - vy) + (yn(vz) - vz)
                 st[w, 8, i] = st[w, 8, i] - par[1, i] * strain
                 eyz.append(strain)
-            grad[1, i] += eyz[0] * eyz[1]
+            grad[1, i] += 2.0 * (f[0] * a[0] + f[1] * a[1] + f[2] * a[2]) + eyz[0] * eyz[1]
 
         pl.when(k == steps - 1)(lambda: go_home(2))
 
-        pl.when(has_prev)(lambda: ahead.wait_recv())
-        pl.when(has_next)(lambda: back.wait_recv())
-        for i in range(3):
-            pair = []
-            for w in range(2):
+        shear = []
+        for w in range(2):
+            pl.when(has_prev)(lambda: v_ahead(k, w).wait_recv())
+            pl.when(has_next)(lambda: v_back(k, w).wait_recv())
+            strains = []
+            for i in range(3):
                 vx = edge[w, 0] if i == 0 else st[w, 0, i - 1]
                 vy0 = rx_v[k, 0, w, 0] if i == 0 else st[w, 1, i - 1]
                 vz0 = rx_v[k, 0, w, 1] if i == 0 else st[w, 2, i - 1]
@@ -469,11 +468,21 @@
                 else:
                     st[w, 6, i - 1] = st[w, 6, i - 1] - par[1, i - 1] * exy
                     st[w, 7, i - 1] = st[w, 7, i - 1] - par[1, i - 1] * exz
-                pair.append((exy, exz))
-            if i > 0:
-                grad[1, i - 1] += pair[0][0] * pair[1][0] + pair[0][1] * pair[1][1]
+                    strains.append((exy, exz))
+            shear.append(strains)
+            pl.when(k < steps - 1)(lambda w=w: transverse(k + 1, w))
+
+        for i in range(2):
+            f, a = shear[0][i], shear[1][i]
+            grad[1, i] += f[0] * a[0] + f[1] * a[1]
         return carry
 
+    for w in range(2):
+        when_all(stays, local_in[w : w + 1], "wait")
+        when_all(moves, wave_swap[w], "wait_recv")
+        when_all(has_prev, edge_next[w], "wait_recv")
+        when_all(has_next, edge_prev[w], "wait_recv")
+        transverse(0, w)
     lax.fori_loop(0, steps, step, 0)
 
     go_home(3)
@@ -530,15 +539,14 @@
         pl.when(jnp.logical_not(own))(lambda t=t: grad_remote(t).wait_send())
 
     def drain(k, carry):
-        back, ahead = v_copies(k)
-        pl.when(has_prev)(lambda: back.wait_send())
-        pl.when(has_next)(lambda: ahead.wait_send())
-
-        @pl.when(k < steps - 1)
-        def _():
-            s_back, s_ahead = s_copies(k)
-            pl.when(has_prev)(lambda: s_back.wait_send())
-            pl.when(has_next)(lambda: s_ahead.wait_send())
+        for w in range(2):
+            pl.when(has_prev)(lambda: v_back(k, w).wait_send())
+            pl.when(has_next)(lambda: v_ahead(k, w).wait_send())
+
+            @pl.when(k < steps - 1)
+            def _(w=w):
+                pl.when(has_prev)(lambda: s_back(k, w).wait_send())
+                pl.when(has_next)(lambda: s_ahead(k, w).wait_send())
 
         return carry
 
@@ -550,15 +558,9 @@
 
     lax.fori_loop(0, n_slab, drain_msg, 0)
 
-    @pl.when(sends_next)
-    def _():
-        for copy in next_copies:
-            copy.wait_send()
-
-    @pl.when(sends_prev)
-    def _():
-        for copy in prev_copies:
-            copy.wait_send()
+    when_all(sends_next, mat_edge + edge_next[0] + edge_next[1], "wait_send")
+    when_all(sends_prev, edge_prev[0] + edge_prev[1], "wait_send")
+    when_all(moves, mat_swap + wave_swap[0] + wave_swap[1], "wait_send")
 
     @pl.when(stays)
     def _():
@@ -567,8 +569,6 @@
 
     @pl.when(moves)
     def _():
-        for copy in swap_in:
-            copy.wait_send()
         for n in range(len(groups)):
             home_away(n).wait_send()
             home_land(n).wait()
@@ -637,10 +637,10 @@
             dma((5,)),
             dma((10,)),
             dma((10,)),
-            dma((steps, 2)),
-            dma((steps, 2)),
-            dma((steps, 2)),
-            dma((steps, 2)),
+            dma((steps, 2, 2)),
+            dma((steps, 2, 2)),
+            dma((steps, 2, 2)),
+            dma((steps, 2, 2)),
             dma((n_slab,)),
             dma((n_slab,)),
             dma((n_shot,)),

time: 50.3 us -> 47.8 us (0.950)
  Pallas kernels: 48.8 us -> 46.3 us
    pallas_call x1, Pallas kernels: 47.1 us -> 44.6 us  [shards(): pl.pallas_call(functools.partial(kernel, n_shot, n_slab, steps), out_shap...]
where the time goes in v4:
time: 47.8 us; the launch traced here: 47.6 us
  Pallas kernels  46.3 us (97%)
  between operations  1.29 us (3%)
    pallas_call x1, Pallas kernels, shards(): pl.pallas_call(functools.partial(kernel, n_shot, n_slab, steps), out_shap...  44.6 us
    pallas_call x1, Pallas kernels, shards(): pl.pallas_call(deliver, out_shape=tuple((jax.ShapeDtypeStruct(o.shape, o....  1.73 us

profile of v4, /device:TPU:11, one launch (start us, length us, event | category | flops | bytes accessed | tf_op | source)
XLA Modules:
  0.0 47.6 jit_solution(60640452109763139)
XLA Ops:
  1.3 44.6 %shard_map.121 = (f32[1,9,2,32,128]{4,3,2,1,0:T(8,128)}, f32[2,8,128]{2,1,0:T(8,128)}, f32[2,8,128]{2,1,0:T(8,128)}) custom-call(f32[2,32,128]{2,1,0:T(8,128)} %lam_hbm.1, f32[2,32,128]{2,1,0:T(8,128)} %mu_hbm.1, f32[2,32,128]{2,1,0:T(8,128)} %buo_hbm.1, f32[1,9,2,32,128]{4,3,2,1,0:T(8,128)} %fwd_hbm.1, f32[1,9,2,32,128]{4,3,2,1,0:T(8,128)} %adj_hbm.1, ...), custom_call_target="tpu_custom_call" | custom-call | flops 10000000 | bytes 1000000 | tf_op jit(solution)/shard_map/pallas_call | solution.py:599
  45.9 1.7 %shard_map.122 = (f32[1,9,2,32,128]{4,3,2,1,0:T(8,128)}, f32[2,8,128]{2,1,0:T(8,128)}, f32[2,8,128]{2,1,0:T(8,128)}) custom-call(f32[1,9,2,32,128]{4,3,2,1,0:T(8,128)} %get-tuple-element.6.a, f32[2,8,128]{2,1,0:T(8,128)} %get-tuple-element.7.b, f32[2,8,128]{2,1,0:T(8,128)} %get-tuple-element.8.c), custom_call_target="tpu_custom_call" | custom-call | bytes 1000000 | tf_op jit(solution)/shard_map/pallas_call | solution.py:667

commit v5 on v4

--- a/solution.py
+++ b/solution.py
@@ -9,6 +9,7 @@
 DT = 0.3
 MESH = pl.DeviceIdType.MESH
 MSG = 16
+LEAD = 2
 
 
 def at_virtual(shot, slab):
@@ -54,6 +55,7 @@
     amp,
     grad,
     rx_grad,
+    kept,
     own,
     own_par,
     home,
@@ -224,7 +226,7 @@
         copy.wait()
     when_all(sends_next, mat_edge, "start")
     when_all(moves, mat_swap, "start")
-    for w in range(2):
+    for w in (1, 0):
         own_in[w].wait()
         when_all(sends_next, edge_next[w], "start")
         when_all(sends_prev, edge_prev[w], "start")
@@ -373,119 +375,143 @@
         pl.when(has_prev)(lambda: v_back(k, w).start())
         pl.when(has_next)(lambda: v_ahead(k, w).start())
 
-    def step(k, carry):
-        normal = []
-        for w in range(2):
-            @pl.when(k > 0)
-            def _(w=w):
-                pl.when(has_prev)(lambda: s_ahead(k, w).wait_recv())
-                pl.when(has_next)(lambda: s_back(k, w).wait_recv())
-
-            sxx = [rx_s[k, 0, w], st[w, 3, 0], st[w, 3, 1], rx_s[k, 1, w]]
-            for i in range(3):
-                sxy = edge[w, 1] if i == 0 else st[w, 6, i - 1]
-                sxz = edge[w, 2] if i == 0 else st[w, 7, i - 1]
-                factor = edge_par[1] if i == 0 else par[2, i - 1]
-                change = factor * ((sxx[i + 1] - sxx[i]) + (sxy - yp(sxy)) + (sxz - zp(sxz)))
-                if i == 0:
-                    edge[w, 0] = edge[w, 0] - change
-                else:
-                    st[w, 0, i - 1] = st[w, 0, i - 1] - change
-
-            terms = []
-            for i in range(2):
-                at = pl.ds(i * ny, ny)
-                gain = amp[k, 0:1] * spot[at] if w == 0 else DT * push[k, at]
-                vx0 = edge[w, 0] if i == 0 else st[w, 0, 0]
-                vy, vz = st[w, 1, i], st[w, 2, i]
-                exx = st[w, 0, i] - vx0
-                eyy = vy - yp(vy)
-                ezz = vz - zp(vz)
-                tr = exx + eyy + ezz
-                common = par[0, i] * tr + gain
-                twice = 2.0 * par[1, i]
-                new = st[w, 3, i] - (common + twice * exx)
-                st[w, 3, i] = new
-                tx_s[k, i, w] = new
-                st[w, 4, i] = st[w, 4, i] - (common + twice * eyy)
-                st[w, 5, i] = st[w, 5, i] - (common + twice * ezz)
-                terms.append((exx, eyy, ezz, tr))
-            normal.append(terms)
-
-            @pl.when(k < steps - 1)
-            def _(w=w):
-                back = remote(
-                    tx_s.at[k, 0, w],
-                    rx_s.at[k + 1, 1, w],
-                    s_send.at[k, 0, w],
-                    s_recv.at[k + 1, 1, w],
-                    prev_dev,
-                )
-                ahead = remote(
-                    tx_s.at[k, 1, w],
-                    rx_s.at[k + 1, 0, w],
-                    s_send.at[k, 1, w],
-                    s_recv.at[k + 1, 0, w],
-                    next_dev,
-                )
-                pl.when(has_prev)(lambda: back.start())
-                pl.when(has_next)(lambda: ahead.start())
-
-        @pl.when(k == steps - 1)
+    def normal(k, w):
+        @pl.when(k > 0)
         def _():
-            go_home(0)
-            go_home(1)
-
+            pl.when(has_prev)(lambda: s_ahead(k, w).wait_recv())
+            pl.when(has_next)(lambda: s_back(k, w).wait_recv())
+
+        sxx = [rx_s[k, 0, w], st[w, 3, 0], st[w, 3, 1], rx_s[k, 1, w]]
+        for i in range(3):
+            sxy = edge[w, 1] if i == 0 else st[w, 6, i - 1]
+            sxz = edge[w, 2] if i == 0 else st[w, 7, i - 1]
+            factor = edge_par[1] if i == 0 else par[2, i - 1]
+            change = factor * ((sxx[i + 1] - sxx[i]) + (sxy - yp(sxy)) + (sxz - zp(sxz)))
+            if i == 0:
+                edge[w, 0] = edge[w, 0] - change
+            else:
+                st[w, 0, i - 1] = st[w, 0, i - 1] - change
+
+        terms = []
         for i in range(2):
-            f, a = normal[0][i], normal[1][i]
-            grad[0, i] += f[3] * a[3]
-            eyz = []
-            for w in range(2):
-                vy, vz = st[w, 1, i], st[w, 2, i]
-                strain = (zn(vy) - vy) + (yn(vz) - vz)
-                st[w, 8, i] = st[w, 8, i] - par[1, i] * strain
-                eyz.append(strain)
-            grad[1, i] += 2.0 * (f[0] * a[0] + f[1] * a[1] + f[2] * a[2]) + eyz[0] * eyz[1]
-
-        pl.when(k == steps - 1)(lambda: go_home(2))
-
-        shear = []
-        for w in range(2):
-            pl.when(has_prev)(lambda: v_ahead(k, w).wait_recv())
-            pl.when(has_next)(lambda: v_back(k, w).wait_recv())
-            strains = []
-            for i in range(3):
-                vx = edge[w, 0] if i == 0 else st[w, 0, i - 1]
-                vy0 = rx_v[k, 0, w, 0] if i == 0 else st[w, 1, i - 1]
-                vz0 = rx_v[k, 0, w, 1] if i == 0 else st[w, 2, i - 1]
-                vy1 = rx_v[k, 1, w, 0] if i == 2 else st[w, 1, i]
-                vz1 = rx_v[k, 1, w, 1] if i == 2 else st[w, 2, i]
-                exy = (yn(vx) - vx) + (vy1 - vy0)
-                exz = (zn(vx) - vx) + (vz1 - vz0)
-                if i == 0:
-                    edge[w, 1] = edge[w, 1] - edge_par[0] * exy
-                    edge[w, 2] = edge[w, 2] - edge_par[0] * exz
-                else:
-                    st[w, 6, i - 1] = st[w, 6, i - 1] - par[1, i - 1] * exy
-                    st[w, 7, i - 1] = st[w, 7, i - 1] - par[1, i - 1] * exz
-                    strains.append((exy, exz))
-            shear.append(strains)
-            pl.when(k < steps - 1)(lambda w=w: transverse(k + 1, w))
+            at = pl.ds(i * ny, ny)
+            gain = amp[k, 0:1] * spot[at] if w == 0 else DT * push[k, at]
+            vx0 = edge[w, 0] if i == 0 else st[w, 0, 0]
+            vy, vz = st[w, 1, i], st[w, 2, i]
+            exx = st[w, 0, i] - vx0
+            eyy = vy - yp(vy)
+            ezz = vz - zp(vz)
+            tr = exx + eyy + ezz
+            common = par[0, i] * tr + gain
+            twice = 2.0 * par[1, i]
+            new = st[w, 3, i] - (common + twice * exx)
+            st[w, 3, i] = new
+            tx_s[k, i, w] = new
+            st[w, 4, i] = st[w, 4, i] - (common + twice * eyy)
+            st[w, 5, i] = st[w, 5, i] - (common + twice * ezz)
+            terms.append((exx, eyy, ezz, tr))
+
+        @pl.when(k < steps - 1)
+        def _():
+            back = remote(
+                tx_s.at[k, 0, w],
+                rx_s.at[k + 1, 1, w],
+                s_send.at[k, 0, w],
+                s_recv.at[k + 1, 1, w],
+                prev_dev,
+            )
+            ahead = remote(
+                tx_s.at[k, 1, w],
+                rx_s.at[k + 1, 0, w],
+                s_send.at[k, 1, w],
+                s_recv.at[k + 1, 0, w],
+                next_dev,
+            )
+            pl.when(has_prev)(lambda: back.start())
+            pl.when(has_next)(lambda: ahead.start())
+
+        if w == 1:
+
+            @pl.when(k == steps - 1)
+            def _():
+                go_home(0)
+                go_home(1)
 
         for i in range(2):
-            f, a = shear[0][i], shear[1][i]
-            grad[1, i] += f[0] * a[0] + f[1] * a[1]
-        return carry
-
-    for w in range(2):
+            vy, vz = st[w, 1, i], st[w, 2, i]
+            eyz = (zn(vy) - vy) + (yn(vz) - vz)
+            st[w, 8, i] = st[w, 8, i] - par[1, i] * eyz
+            exx, eyy, ezz, tr = terms[i]
+            if w == 1:
+                for n, strain in enumerate((exx, eyy, ezz, eyz)):
+                    kept[k, n, i] = strain
+            else:
+                a = [kept[k, n, i] for n in range(4)]
+                grad[0, i] += tr * (a[0] + a[1] + a[2])
+                grad[1, i] += 2.0 * (exx * a[0] + eyy * a[1] + ezz * a[2]) + eyz * a[3]
+        if w == 1:
+            pl.when(k == steps - 1)(lambda: go_home(2))
+
+    def sheared(k, w):
+        pl.when(has_prev)(lambda: v_ahead(k, w).wait_recv())
+        pl.when(has_next)(lambda: v_back(k, w).wait_recv())
+        strains = []
+        for i in range(3):
+            vx = edge[w, 0] if i == 0 else st[w, 0, i - 1]
+            vy0 = rx_v[k, 0, w, 0] if i == 0 else st[w, 1, i - 1]
+            vz0 = rx_v[k, 0, w, 1] if i == 0 else st[w, 2, i - 1]
+            vy1 = rx_v[k, 1, w, 0] if i == 2 else st[w, 1, i]
+            vz1 = rx_v[k, 1, w, 1] if i == 2 else st[w, 2, i]
+            exy = (yn(vx) - vx) + (vy1 - vy0)
+            exz = (zn(vx) - vx) + (vz1 - vz0)
+            if i == 0:
+                edge[w, 1] = edge[w, 1] - edge_par[0] * exy
+                edge[w, 2] = edge[w, 2] - edge_par[0] * exz
+            else:
+                st[w, 6, i - 1] = st[w, 6, i - 1] - par[1, i - 1] * exy
+                st[w, 7, i - 1] = st[w, 7, i - 1] - par[1, i - 1] * exz
+                strains.append((exy, exz))
+        pl.when(k < steps - 1)(lambda: transverse(k + 1, w))
+        for i in range(2):
+            exy, exz = strains[i]
+            if w == 1:
+                kept[k, 4, i] = exy
+                kept[k, 5, i] = exz
+            else:
+                grad[1, i] += exy * kept[k, 4, i] + exz * kept[k, 5, i]
+        if w == 1:
+            pl.when(k == steps - 1)(lambda: go_home(3))
+
+    def arrive(w):
         when_all(stays, local_in[w : w + 1], "wait")
         when_all(moves, wave_swap[w], "wait_recv")
         when_all(has_prev, edge_next[w], "wait_recv")
         when_all(has_next, edge_prev[w], "wait_recv")
         transverse(0, w)
-    lax.fori_loop(0, steps, step, 0)
-
-    go_home(3)
+
+    def adjoint_only(k, carry):
+        normal(k, 1)
+        sheared(k, 1)
+        return carry
+
+    def both(k, carry):
+        normal(k, 1)
+        normal(k - LEAD, 0)
+        sheared(k, 1)
+        sheared(k - LEAD, 0)
+        return carry
+
+    def forward_only(k, carry):
+        normal(k, 0)
+        sheared(k, 0)
+        return carry
+
+    arrive(1)
+    lax.fori_loop(0, LEAD, adjoint_only, 0)
+    arrive(0)
+    lax.fori_loop(LEAD, steps, both, 0)
+    lax.fori_loop(steps - LEAD, steps, forward_only, 0)
+
     grad[...] = DT * grad[...]
     part = ny // n_shot
 
@@ -508,6 +534,12 @@
         @pl.when(own)
         def _(t=t):
             rx_grad[t] = grad[:, :, t * part : (t + 1) * part]
+
+    @pl.when(moves)
+    def _():
+        for n in range(len(groups)):
+            home_away(n).wait_recv()
+            home_land(n).start()
 
     for t in range(n_shot):
         own = jnp.logical_and(stays, t == shot)
@@ -521,12 +553,6 @@
                 grad_recv.at[t],
                 (jnp.int32(t), my_slab),
             ).wait_recv()
-
-    @pl.when(moves)
-    def _():
-        for n in range(len(groups)):
-            home_away(n).wait_recv()
-            home_land(n).start()
 
     total = rx_grad[0]
     for t in range(1, n_shot):
@@ -627,6 +653,7 @@
             pltpu.VMEM((steps, 8, nz), f32),
             pltpu.VMEM((2, planes, ny, nz), f32),
             pltpu.VMEM((n_shot, 2, planes, part, nz), f32),
+            pltpu.VMEM((steps, 6, planes, ny, nz), f32),
             pltpu.VMEM((2, 9, planes, ny, nz), f32),
             pltpu.VMEM((3, planes, ny, nz), f32),
             pltpu.VMEM((9, planes, ny, nz), f32),

time: 47.8 us -> 49.4 us (1.033); the launches traced: 47.6 us -> 48.5 us
  Pallas kernels: 46.3 us -> 47.2 us
    pallas_call x1, Pallas kernels: 44.6 us -> 45.5 us  [shards(): pl.pallas_call(functools.partial(kernel, n_shot, n_slab, steps), out_shap...]
where the time goes in v5:
time: 49.4 us; the launch traced here: 48.5 us
  Pallas kernels  47.2 us (96%)
  between operations  1.29 us (3%)
    pallas_call x1, Pallas kernels, shards(): pl.pallas_call(functools.partial(kernel, n_shot, n_slab, steps), out_shap...  45.5 us
    pallas_call x1, Pallas kernels, shards(): pl.pallas_call(deliver, out_shape=tuple((jax.ShapeDtypeStruct(o.shape, o....  1.73 us

profile of v5, /device:TPU:11, one launch (start us, length us, event | category | flops | bytes accessed | tf_op | source)
XLA Modules:
  0.0 48.5 jit_solution(107830813808502112)
XLA Ops:
  1.3 45.5 %shard_map.121 = (f32[1,9,2,32,128]{4,3,2,1,0:T(8,128)}, f32[2,8,128]{2,1,0:T(8,128)}, f32[2,8,128]{2,1,0:T(8,128)}) custom-call(f32[2,32,128]{2,1,0:T(8,128)} %lam_hbm.1, f32[2,32,128]{2,1,0:T(8,128)} %mu_hbm.1, f32[2,32,128]{2,1,0:T(8,128)} %buo_hbm.1, f32[1,9,2,32,128]{4,3,2,1,0:T(8,128)} %fwd_hbm.1, f32[1,9,2,32,128]{4,3,2,1,0:T(8,128)} %adj_hbm.1, ...), custom_call_target="tpu_custom_call" | custom-call | flops 10000000 | bytes 1000000 | tf_op jit(solution)/shard_map/pallas_call | solution.py:625
  46.8 1.7 %shard_map.122 = (f32[1,9,2,32,128]{4,3,2,1,0:T(8,128)}, f32[2,8,128]{2,1,0:T(8,128)}, f32[2,8,128]{2,1,0:T(8,128)}) custom-call(f32[1,9,2,32,128]{4,3,2,1,0:T(8,128)} %get-tuple-element.6.a, f32[2,8,128]{2,1,0:T(8,128)} %get-tuple-element.7.b, f32[2,8,128]{2,1,0:T(8,128)} %get-tuple-element.8.c), custom_call_target="tpu_custom_call" | custom-call | bytes 1000000 | tf_op jit(solution)/shard_map/pallas_call | solution.py:694

commit v6 on v4

--- a/solution.py
+++ b/solution.py
@@ -283,15 +283,8 @@
             push[k] += out[k * rows : (k + 1) * rows] + out[(steps + k) * rows : (steps + k + 1) * rows]
         return carry
 
-    lax.fori_loop(0, n_slab // 2, scatter, 0)
-
-    head = rx_msg[my_slab]
-    source = head[steps + 3 : steps + 4].astype(jnp.int32) - my_slab * cells
-    flat = lax.broadcasted_iota(jnp.int32, (rows, nz), 0) * nz
-    flat = flat + lax.broadcasted_iota(jnp.int32, (rows, nz), 1)
-    spot[...] = (flat == source).astype(jnp.float32)
-    for k in range(steps):
-        amp[k] = jnp.broadcast_to(DT * head[steps + 2 : steps + 3, k : k + 1], (8, nz))
+    blocks = n_slab // 2
+    lax.fori_loop(0, blocks - 2, scatter, 0)
 
     when_all(stays, local_in[2:], "wait")
     when_all(moves, mat_swap, "wait_recv")
@@ -483,6 +476,15 @@
         when_all(has_prev, edge_next[w], "wait_recv")
         when_all(has_next, edge_prev[w], "wait_recv")
         transverse(0, w)
+        lax.fori_loop(blocks - 2 + w, blocks - 1 + w, scatter, 0)
+    head = rx_msg[my_slab]
+    source = head[steps + 3 : steps + 4].astype(jnp.int32) - my_slab * cells
+    flat = lax.broadcasted_iota(jnp.int32, (rows, nz), 0) * nz
+    flat = flat + lax.broadcasted_iota(jnp.int32, (rows, nz), 1)
+    spot[...] = (flat == source).astype(jnp.float32)
+    for k in range(steps):
+        amp[k] = jnp.broadcast_to(DT * head[steps + 2 : steps + 3, k : k + 1], (8, nz))
+
     lax.fori_loop(0, steps, step, 0)
 
     go_home(3)
@@ -508,6 +510,12 @@
         @pl.when(own)
         def _(t=t):
             rx_grad[t] = grad[:, :, t * part : (t + 1) * part]
+
+    @pl.when(moves)
+    def _():
+        for n in range(len(groups)):
+            home_away(n).wait_recv()
+            home_land(n).start()
 
     for t in range(n_shot):
         own = jnp.logical_and(stays, t == shot)
@@ -521,12 +529,6 @@
                 grad_recv.at[t],
                 (jnp.int32(t), my_slab),
             ).wait_recv()
-
-    @pl.when(moves)
-    def _():
-        for n in range(len(groups)):
-            home_away(n).wait_recv()
-            home_land(n).start()
 
     total = rx_grad[0]
     for t in range(1, n_shot):

time: 47.8 us -> 47.5 us (level)
  Pallas kernels: 46.3 us -> 45.8 us
where the time goes in v6:
time: 47.5 us; the launch traced here: 47.1 us
  Pallas kernels  45.8 us (96%)
  between operations  1.29 us (3%)
    pallas_call x1, Pallas kernels, shards(): pl.pallas_call(functools.partial(kernel, n_shot, n_slab, steps), out_shap...  44.1 us
    pallas_call x1, Pallas kernels, shards(): pl.pallas_call(deliver, out_shape=tuple((jax.ShapeDtypeStruct(o.shape, o....  1.73 us

profile of v6, /device:TPU:11, one launch (start us, length us, event | category | flops | bytes accessed | tf_op | source)
XLA Modules:
  0.0 47.1 jit_solution(5797625763772729740)
XLA Ops:
  1.3 44.1 %shard_map.121 = (f32[1,9,2,32,128]{4,3,2,1,0:T(8,128)}, f32[2,8,128]{2,1,0:T(8,128)}, f32[2,8,128]{2,1,0:T(8,128)}) custom-call(f32[2,32,128]{2,1,0:T(8,128)} %lam_hbm.1, f32[2,32,128]{2,1,0:T(8,128)} %mu_hbm.1, f32[2,32,128]{2,1,0:T(8,128)} %buo_hbm.1, f32[1,9,2,32,128]{4,3,2,1,0:T(8,128)} %fwd_hbm.1, f32[1,9,2,32,128]{4,3,2,1,0:T(8,128)} %adj_hbm.1, ...), custom_call_target="tpu_custom_call" | custom-call | flops 10000000 | bytes 1000000 | tf_op jit(solution)/shard_map/pallas_call | solution.py:601
  45.4 1.7 %shard_map.122 = (f32[1,9,2,32,128]{4,3,2,1,0:T(8,128)}, f32[2,8,128]{2,1,0:T(8,128)}, f32[2,8,128]{2,1,0:T(8,128)}) custom-call(f32[1,9,2,32,128]{4,3,2,1,0:T(8,128)} %get-tuple-element.6.a, f32[2,8,128]{2,1,0:T(8,128)} %get-tuple-element.7.b, f32[2,8,128]{2,1,0:T(8,128)} %get-tuple-element.8.c), custom_call_target="tpu_custom_call" | custom-call | bytes 1000000 | tf_op jit(solution)/shard_map/pallas_call | solution.py:669
